TPU v7x, 32 devices: a whole 2x2x4 slice. The times are simulated.
32 devices in a mesh: group: 2 (over y), seq: 4 (over z), dp: 2 (over x), head: 2 (over core).
Axes of the slice: x: 2, y: 2, z: 4, core: 2. Of those that a mesh axis runs over, the one named last changes fastest.
Arguments:
- gdn_query: bfloat16 [4, 512, 2048], P(('group', 'dp'), 'seq', 'head'), parts along dimension 0, may hold values from -6 to 6
- gdn_key: bfloat16 [4, 512, 2048], P(('group', 'dp'), 'seq', 'head'), parts along dimension 0, may hold values from -6 to 6
- gdn_value: bfloat16 [4, 512, 2048], P(('group', 'dp'), 'seq', 'head'), parts along dimension 0, may hold values from -6 to 6
- gdn_cot: bfloat16 [4, 512, 2048], P(('group', 'dp'), 'seq', 'head'), parts along dimension 0, may hold values from -6 to 6
- gate_log: float32 [4, 16, 512], P(('group', 'dp'), 'head', 'seq'), parts along dimension 0, may hold values from -1 to 0, as said below
- beta: float32 [4, 16, 512], P(('group', 'dp'), 'head', 'seq'), parts along dimension 0, may hold values from 0 to 1
- state_in: float32 [4, 4, 16, 128, 128], P(('group', 'dp'), 'seq', 'head'), parts along dimension 0, may hold values from -3 to 3
- gdn_rot: bfloat16 [16, 128, 128], P('head'), may hold values from -0.5 to 0.5
- att_query: bfloat16 [4, 512, 2048], P(('group', 'dp'), 'seq', 'head'), parts along dimension 0, may hold values from -130 to 130
- att_key: bfloat16 [4, 512, 1024], P(('group', 'dp'), 'seq', 'head'), parts along dimension 0, may hold values from -7 to 7
- att_value: bfloat16 [4, 512, 1024], P(('group', 'dp'), 'seq', 'head'), parts along dimension 0, may hold values from -6 to 6
- att_cot: bfloat16 [4, 512, 2048], P(('group', 'dp'), 'seq', 'head'), parts along dimension 0, may hold values from -6 to 6
- att_rot: bfloat16 [16, 128, 128], P('head'), may hold values from -0.5 to 0.5
Outputs:
- gdn_query_grad: bfloat16 [4, 512, 2048], P(('group', 'dp'), 'seq', 'head'), parts along dimension 0
- gdn_key_grad: bfloat16 [4, 512, 2048], P(('group', 'dp'), 'seq', 'head'), parts along dimension 0
- gdn_value_grad: bfloat16 [4, 512, 2048], P(('group', 'dp'), 'seq', 'head'), parts along dimension 0
- gate_grad: float32 [4, 16, 512], P(('group', 'dp'), 'head', 'seq'), parts along dimension 0
- beta_grad: float32 [4, 16, 512], P(('group', 'dp'), 'head', 'seq'), parts along dimension 0
- gdn_rot_grad: float32 [32, 128, 128], P(('group', 'head'), 'dp'), parts along dimension 0
- att_query_grad: bfloat16 [4, 512, 2048], P(('group', 'dp'), 'seq', 'head'), parts along dimension 0
- att_key_grad: bfloat16 [4, 512, 1024], P(('group', 'dp'), 'seq', 'head'), parts along dimension 0
- att_value_grad: bfloat16 [4, 512, 1024], P(('group', 'dp'), 'seq', 'head'), parts along dimension 0
- att_rot_grad: float32 [32, 128, 128], P(('group', 'head'), 'dp'), parts along dimension 0
There are 2 independent parts, one for each index of `group`. A program takes and returns all parts, laid end to end along the dimension named above; an argument that names none is the same for every part. Nothing has to cross between parts.
Inputs may be any that keep to these rules, and one draw needn't show every extreme that they name: gate_log is never positive.
All inputs are finite; a program needn't handle non-finite values.
Results may differ from a plain program's by a relative error of at most 0.008.
Values may be sent and summed in bfloat16 or wider, within the bound.
A program may use at most 192 MiB of HBM per device.

v0:
```python
import jax
import jax.numpy as jnp
from jax import lax
from jax.sharding import PartitionSpec as P

WINDOW = 256
STRETCH = 64


NORM_EPSILON = 1e-06
HIGHEST_PRECISION = lax.Precision.HIGHEST
MASK_FLOOR = -1e30


def entering(x, axis, combine, identity):
    size, position = (lax.axis_size(axis), lax.axis_index(axis))
    everything = jax.tree.map(lambda part: lax.all_gather(part, axis), x)
    start = jax.tree.map(
        lambda part, zero: jnp.broadcast_to(jnp.asarray(zero, part.dtype), part.shape), x, identity
    )

    def lap(k, before):
        at = size - 1 - k
        reached = at > position
        new = combine(before, jax.tree.map(lambda part: part[at], everything))
        return jax.tree.map(lambda a, b: jnp.where(reached, a, b), new, before)

    return lax.fori_loop(0, size, lap, start)


def from_behind(x, axis, by):
    size = lax.axis_size(axis)
    pairs = [(i, i + by) for i in range(size) if 0 <= i + by < size]
    return lax.ppermute(x, axis, pairs)


def unit_rows(values):
    return values / jnp.sqrt(jnp.sum(values * values, axis=-1, keepdims=True) + NORM_EPSILON)


def stretch_delta(start_state, query_in, key_in, value_in, gate_in, beta_in):
    query_unit = unit_rows(query_in)
    key_unit = unit_rows(key_in)
    seq_rows, head_count, tok_rows, head_dim = query_in.shape
    blocks = tok_rows // STRETCH

    def split_blocks(array):
        shaped = array.reshape((seq_rows, head_count, blocks, STRETCH) + array.shape[3:])
        return jnp.moveaxis(shaped, 2, 0)

    positions = jnp.arange(STRETCH)
    strict = positions[:, None] > positions[None, :]
    within = positions[:, None] >= positions[None, :]
    identity = jnp.eye(STRETCH, dtype=jnp.float32)

    def advance(state_now, pieces):
        query_part, key_part, value_part, gate_part, beta_part = pieces
        decay_sum = jnp.cumsum(gate_part, axis=-1)
        gap_sums = decay_sum[..., :, None] - decay_sum[..., None, :]
        ratios = jnp.where(within, jnp.exp(jnp.where(within, gap_sums, 0.0)), 0.0)
        key_key = jnp.einsum("bhtk,bhsk->bhts", key_part, key_part, precision=HIGHEST_PRECISION)
        lower_part = jnp.where(strict, beta_part[..., :, None] * ratios * key_key, 0.0)
        state_seen = jnp.einsum("bhtk,bhvk->bhtv", key_part, state_now, precision=HIGHEST_PRECISION)
        decay_now = jnp.exp(decay_sum)
        target = beta_part[..., None] * (value_part - decay_now[..., None] * state_seen)
        written = jax.scipy.linalg.solve_triangular(
            identity + lower_part, target, lower=True, unit_diagonal=True
        )
        query_key = jnp.einsum("bhtk,bhsk->bhts", query_part, key_part, precision=HIGHEST_PRECISION)
        from_state = jnp.einsum(
            "bhtk,bhvk->bhtv", query_part, state_now, precision=HIGHEST_PRECISION
        )
        outputs = decay_now[..., None] * from_state + jnp.einsum(
            "bhts,bhsv->bhtv", ratios * query_key, written, precision=HIGHEST_PRECISION
        )
        last_sum = decay_sum[..., -1:]
        carried_keys = jnp.exp(last_sum - decay_sum)[..., None] * key_part
        next_state = jnp.exp(last_sum)[..., None] * state_now + jnp.einsum(
            "bhsv,bhsk->bhvk", written, carried_keys, precision=HIGHEST_PRECISION
        )
        return (next_state, outputs)

    members = tuple(
        (split_blocks(member) for member in (query_unit, key_unit, value_in, gate_in, beta_in))
    )
    final_state, outputs = lax.scan(advance, start_state, members)
    outputs = jnp.moveaxis(outputs, 0, 2).reshape(seq_rows, head_count, tok_rows, head_dim)
    return (outputs, final_state)


def delta_backward(gdn_query, gdn_key, gdn_value, gdn_cot, gate_log, beta, state_in, gdn_rot):
    seq_rows, tok_rows, row_width = gdn_query.shape
    head_count = gdn_rot.shape[0]
    head_dim = gdn_rot.shape[1]

    def heads_first(array):
        return jnp.transpose(
            array.reshape(seq_rows, tok_rows, head_count, head_dim), (0, 2, 1, 3)
        ).astype(jnp.float32)

    cotangent = gdn_cot.reshape(seq_rows, tok_rows, head_count, head_dim)
    out_grad = jnp.einsum(
        "stha,hab->sthb", cotangent, gdn_rot, preferred_element_type=jnp.float32
    ).astype(jnp.bfloat16)
    out_grad = jnp.transpose(out_grad, (0, 2, 1, 3)).astype(jnp.float32)
    query_first = heads_first(gdn_query)
    key_first = heads_first(gdn_key)
    value_first = heads_first(gdn_value)
    primal, pullback = jax.vjp(
        stretch_delta, state_in[:, 0], query_first, key_first, value_first, gate_log, beta
    )
    outputs, final_state = primal
    local_state = pullback((out_grad, jnp.zeros_like(final_state)))[0]
    identity = jnp.broadcast_to(jnp.eye(head_dim, dtype=jnp.float32), final_state.shape)
    transfer = stretch_delta(
        identity, query_first, key_first, jnp.zeros_like(value_first), gate_log, beta
    )[1]
    transfer = jnp.swapaxes(transfer, -1, -2)

    def compose_blocks(earlier, later):
        joined = jnp.matmul(earlier[0], later[0], precision=HIGHEST_PRECISION)
        offset = jnp.matmul(earlier[1], later[0], precision=HIGHEST_PRECISION) + later[1]
        return (joined, offset)

    incoming = entering(
        (transfer, local_state), "seq", compose_blocks, (identity, jnp.zeros_like(final_state))
    )
    all_part = pullback((out_grad, incoming[1]))

    def tokens_last(array):
        return (
            jnp.transpose(array, (0, 2, 1, 3))
            .reshape(seq_rows, tok_rows, row_width)
            .astype(jnp.bfloat16)
        )

    rounded_out = jnp.transpose(outputs, (0, 2, 1, 3)).astype(jnp.bfloat16)
    rot_term = jnp.einsum(
        "stha,sthb->hab", cotangent, rounded_out, preferred_element_type=jnp.float32
    )
    query_grad = tokens_last(all_part[1])
    key_grad = tokens_last(all_part[2])
    value_grad = tokens_last(all_part[3])
    return (query_grad, key_grad, value_grad, all_part[4], all_part[5], rot_term)


def window_backward(att_query, att_key, att_value, att_cot, att_rot):
    seq_rows, tok_rows, row_width = att_query.shape
    head_count = att_rot.shape[0]
    head_dim = att_rot.shape[1]
    kv_width = att_key.shape[2]
    kv_count = kv_width // head_dim
    group_size = head_count // kv_count
    reach_shards = -(-WINDOW // tok_rows)
    key_span = (reach_shards + 1) * tok_rows
    seq_place = lax.axis_index("seq")
    own_gate_pair = jnp.stack([att_key, att_value])
    gathered = []
    for distance in range(reach_shards, 0, -1):
        gathered.append(from_behind(own_gate_pair, "seq", distance))
    gathered.append(own_gate_pair)
    window_pair = jnp.concatenate(gathered, axis=2)
    keys_window = window_pair[0].reshape(seq_rows, key_span, kv_count, head_dim)
    values_window = window_pair[1].reshape(seq_rows, key_span, kv_count, head_dim)
    queries = att_query.reshape(seq_rows, tok_rows, kv_count, group_size, head_dim)
    cotangent = att_cot.reshape(seq_rows, tok_rows, kv_count, group_size, head_dim)
    rotation = att_rot.reshape(kv_count, group_size, head_dim, head_dim)
    out_grad = jnp.einsum(
        "stkga,kgab->stkgb", cotangent, rotation, preferred_element_type=jnp.float32
    ).astype(jnp.bfloat16)
    score_scale = head_dim ** (-0.5)
    scores = score_scale * jnp.einsum(
        "btkgd,bukd->bkgtu", queries, keys_window, preferred_element_type=jnp.float32
    )
    query_pos = seq_place * tok_rows + jnp.arange(tok_rows, dtype=jnp.int32)
    key_pos = (seq_place - reach_shards) * tok_rows + jnp.arange(key_span, dtype=jnp.int32)
    allowed = (
        (key_pos[None, :] <= query_pos[:, None])
        & (key_pos[None, :] > query_pos[:, None] - WINDOW)
        & (key_pos[None, :] >= 0)
    )
    scores = jnp.where(allowed, scores, MASK_FLOOR)
    row_top = jnp.max(scores, axis=-1, keepdims=True)
    weights = jnp.exp(scores - row_top)
    softmax_rows = weights / jnp.sum(weights, axis=-1, keepdims=True)
    probs_low = softmax_rows.astype(jnp.bfloat16)
    output = jnp.einsum(
        "bkgtu,bukd->btkgd", probs_low, values_window, preferred_element_type=jnp.float32
    )
    prob_grad = jnp.einsum(
        "btkgd,bukd->bkgtu", out_grad, values_window, preferred_element_type=jnp.float32
    )
    row_dot = jnp.sum(softmax_rows * prob_grad, axis=-1, keepdims=True)
    dscore_low = (softmax_rows * (prob_grad - row_dot)).astype(jnp.bfloat16)
    query_grad = (
        score_scale
        * jnp.einsum(
            "bkgtu,bukd->btkgd", dscore_low, keys_window, preferred_element_type=jnp.float32
        )
    ).astype(jnp.bfloat16)
    key_terms = (
        score_scale
        * jnp.einsum("bkgtu,btkgd->bukd", dscore_low, queries, preferred_element_type=jnp.float32)
    ).astype(jnp.bfloat16)
    value_terms = jnp.einsum(
        "bkgtu,btkgd->bukd", probs_low, out_grad, preferred_element_type=jnp.float32
    ).astype(jnp.bfloat16)
    term_pair = jnp.stack([key_terms, value_terms]).reshape(2, seq_rows, key_span, kv_width)
    summed = term_pair[:, :, reach_shards * tok_rows :, :].astype(jnp.float32)
    for distance in range(1, reach_shards + 1):
        piece_rows = term_pair[
            :, :, (reach_shards - distance) * tok_rows : (reach_shards - distance + 1) * tok_rows, :
        ]
        summed = summed + from_behind(piece_rows, "seq", -distance).astype(jnp.float32)
    rot_term = jnp.einsum(
        "stkga,stkgb->kgab",
        cotangent,
        output.astype(jnp.bfloat16),
        preferred_element_type=jnp.float32,
    )
    rot_term = rot_term.reshape(head_count, head_dim, head_dim)
    return (
        query_grad.reshape(seq_rows, tok_rows, row_width),
        summed[0].astype(jnp.bfloat16),
        summed[1].astype(jnp.bfloat16),
        rot_term,
    )


def body(
    gdn_query,
    gdn_key,
    gdn_value,
    gdn_cot,
    gate_log,
    beta,
    state_in,
    gdn_rot,
    att_query,
    att_key,
    att_value,
    att_cot,
    att_rot,
):
    gdn_results = delta_backward(
        gdn_query, gdn_key, gdn_value, gdn_cot, gate_log, beta, state_in, gdn_rot
    )
    att_results = window_backward(att_query, att_key, att_value, att_cot, att_rot)
    gdn_rot_term = gdn_results[5]
    att_rot_term = att_results[3]
    totals = lax.psum((gdn_rot_term, att_rot_term), "seq")
    shares = (
        lax.psum_scatter(totals[0], "dp", scatter_dimension=1, tiled=True),
        lax.psum_scatter(totals[1], "dp", scatter_dimension=1, tiled=True),
    )
    return (
        gdn_results[0],
        gdn_results[1],
        gdn_results[2],
        gdn_results[3],
        gdn_results[4],
        shares[0],
        att_results[0],
        att_results[1],
        att_results[2],
        shares[1],
    )


def solution(mesh):
    placed = (
        P(("group", "dp"), "seq", "head"),
        P(("group", "dp"), "seq", "head"),
        P(("group", "dp"), "seq", "head"),
        P(("group", "dp"), "seq", "head"),
        P(("group", "dp"), "head", "seq"),
        P(("group", "dp"), "head", "seq"),
        P(("group", "dp"), "seq", "head", None, None),
        P("head", None, None),
        P(("group", "dp"), "seq", "head"),
        P(("group", "dp"), "seq", "head"),
        P(("group", "dp"), "seq", "head"),
        P(("group", "dp"), "seq", "head"),
        P("head", None, None),
    )
    return jax.shard_map(
        body,
        mesh=mesh,
        in_specs=placed,
        out_specs=(
            P(("group", "dp"), "seq", "head"),
            P(("group", "dp"), "seq", "head"),
            P(("group", "dp"), "seq", "head"),
            P(("group", "dp"), "head", "seq"),
            P(("group", "dp"), "head", "seq"),
            P(("group", "head"), "dp", None),
            P(("group", "dp"), "seq", "head"),
            P(("group", "dp"), "seq", "head"),
            P(("group", "dp"), "seq", "head"),
            P(("group", "head"), "dp", None),
        ),
        check_vma=False,
    )
```

profile of v0, /device:TPU:0, one launch (start us, length us, event | category | flops | bytes accessed | tf_op | source)
XLA Modules:
  0.0 675.1 jit_solution(17557495839499741473)
XLA Ops:
  10.2 6.6 collective-permute-start
  16.8 4.2 collective-permute-start.1
  29.4 112.8 %while.134 = (s32[]{:T(128)}, f32[1,8,128,128]{3,2,1,0:T(8,128)S(1)}, bf16[2,1,8,64,128]{4,3,0,2,1:T(8,128)(2,1)}, f32[2,1,8,64,64]{4,3,2,1,0:T(8,128)}, f32[2,1...) while((s32[]{:T(128)}, ...), condition=%wide.region_7.9_spmd.clone.clone, body=%wide.region_5.8_spmd.clone.clone.sunk | while | flops 505041984 | bytes 35006800 | solution.py:86
  30.8 1.3 bitcast_dynamic-update-slice_fusion.21
  33.2 40.7 %custom-call.53 = f32[8,1,64,64]{2,3,1,0:T(8,128)} custom-call(f32[8,1,64,64]{3,2,1,0:T(8,128)} %get-tuple-element.3233), custom_call_target="InvertDiagBlocksLowerTriangular" | custom-call | tf_op jit(solution)/shard_map/jvp()/while/body/eval_jaxpr/jit(_solve_triangular)/vmap()/triangular_solve/custom-call.1 | solution.py:66
  74.1 3.0 bitcast_dynamic-update-slice_fusion.19
  87.2 1.3 bitcast_dynamic-update-slice_fusion.21
  89.6 40.7 %custom-call.53 = f32[8,1,64,64]{2,3,1,0:T(8,128)} custom-call(f32[8,1,64,64]{3,2,1,0:T(8,128)} %get-tuple-element.3233), custom_call_target="InvertDiagBlocksLowerTriangular" | custom-call | tf_op jit(solution)/shard_map/jvp()/while/body/eval_jaxpr/jit(_solve_triangular)/vmap()/triangular_solve/custom-call.1 | solution.py:66
  130.6 3.0 bitcast_dynamic-update-slice_fusion.19
  143.4 1.3 convolution_bitcast_fusion.16
  146.8 1.8 reshape.1727
  151.6 1.9 fusion.241
  154.9 3.8 reduce-scatter.3.cloned.1.call-done
  158.7 16.9 %reduce-scatter.5.cloned.1.call-done = f32[8,64,128]{2,1,0:T(8,128)} async-done(((f32[8,128,128]{2,1,0:T(8,128)}), f32[8,64,128]{2,1,0:T(8,128)}) %reduce-scatter.5.cloned.1.call-update) | async-done | bytes 262160 | tf_op jit(solution)/shard_map/reduce_scatter | solution.py:254
  176.0 93.8 %while.136 = (s32[]{:T(128)}, f32[1,8,128,128]{3,2,1,0:T(8,128)S(1)}, f32[2,1,8,1,1]{2,4,3,1,0:T(1,128)S(1)}, f32[2,1,8,64,1]{3,2,4,1,0:T(8,128)S(1)}, f32[2,1,8...) while((s32[]{:T(128)}, ...), condition=%wide.region_9.12_spmd.clone, body=%wide.region_8.11_spmd.clone.sunk | while | flops 403714112 | bytes 6221543 | solution.py:86
  176.0 2.1 convolution_bitcast_fusion.27
  178.6 1.7 fusion.448
  180.2 40.0 %custom-call.56 = f32[8,1,64,64]{2,3,1,0:T(8,128)S(1)} custom-call(f32[8,1,64,64]{3,2,1,0:T(8,128)} %fusion.448), custom_call_target="InvertDiagBlocksLowerTriangular" | custom-call | tf_op jit(solution)/shard_map/transpose(jvp())/while/body/eval_jaxpr/jit(_solve_triangular)/vmap()/triangular_solve/custom-call.0 | solution.py:66
  222.9 2.1 convolution_bitcast_fusion.27
  225.5 1.7 fusion.448
  227.2 40.0 %custom-call.56 = f32[8,1,64,64]{2,3,1,0:T(8,128)S(1)} custom-call(f32[8,1,64,64]{3,2,1,0:T(8,128)} %fusion.448), custom_call_target="InvertDiagBlocksLowerTriangular" | custom-call | tf_op jit(solution)/shard_map/transpose(jvp())/while/body/eval_jaxpr/jit(_solve_triangular)/vmap()/triangular_solve/custom-call.0 | solution.py:66
  270.7 87.0 %while.133 = (s32[]{:T(128)}, f32[1,8,128,128]{3,2,1,0:T(8,128)S(1)}, f32[2,1,8,64]{3,2,1,0:T(8,128)S(1)}, f32[2,1,8,64]{3,2,1,0:T(8,128)S(1)}, f32[2,1,8,64,128]{4,3,2,1,0:T(8,128)S(1)}, /*index=5*/s32[]{:T(128)}, f32[]{:T(128)}) while((s32[]{:T(128)}, f32[1,8,128,128]{3,2,1,0:T(8,128)S(1)}, ...), condition=%wide.region_3.5_spmd.clone.clone, body=%wide.region_1.4_spmd.clone.clone.sunk | while | flops 302870592 | bytes 3849445 | solution.py:86
  273.1 39.3 %custom-call.52 = f32[8,1,64,64]{2,3,1,0:T(8,128)S(1)} custom-call(f32[8,1,64,64]{3,2,1,0:T(8,128)S(1)} %fusion.385), custom_call_target="InvertDiagBlocksLowerTriangular" | custom-call | tf_op jit(solution)/shard_map/while/body/eval_jaxpr/jit(_solve_triangular)/vmap()/triangular_solve/custom-call.1 | solution.py:66
  316.6 39.3 %custom-call.52 = f32[8,1,64,64]{2,3,1,0:T(8,128)S(1)} custom-call(f32[8,1,64,64]{3,2,1,0:T(8,128)S(1)} %fusion.385), custom_call_target="InvertDiagBlocksLowerTriangular" | custom-call | tf_op jit(solution)/shard_map/while/body/eval_jaxpr/jit(_solve_triangular)/vmap()/triangular_solve/custom-call.1 | solution.py:66
  359.2 2.1 fusion.228
  363.2 1.9 fusion.235
  366.1 1.3 collective-permute-start.2
  367.4 1.3 collective-permute-start.3
  368.8 2.3 fusion.236
  371.1 1.8 copy.254
  372.9 14.8 %collective-permute-done.2 = bf16[2,1,128,512]{3,2,1,0:T(8,128)(2,1)} collective-permute-done((bf16[2,1,128,512]{3,2,1,0:T(8,128)(2,1)}, bf16[2,1,128,512]{3,2,1,0:T(8,128)(2,1)}, u32[]{:S(2)}, u32[]{:S(2)}) %collective-permute-start.2) | collective-permute-done | bytes 262176 | tf_op jit(solution)/shard_map/ppermute | solution.py:34
  387.6 28.8 %collective-permute-done.3 = bf16[2,1,128,512]{3,2,1,0:T(8,128)(2,1)} collective-permute-done((bf16[2,1,128,512]{3,2,1,0:T(8,128)(2,1)}, bf16[2,1,128,512]{3,2,1,0:T(8,128)(2,1)}, u32[]{:S(2)}, u32[]{:S(2)}) %collective-permute-start.3) | collective-permute-done | bytes 262176 | tf_op jit(solution)/shard_map/ppermute | solution.py:34
  418.3 1.7 copy.253
  420.0 1.7 all-gather.5.cloned.1.call-done
  421.7 13.7 %while.137 = (s32[]{:T(128)}, f32[1,8,128,128]{2,3,1,0:T(8,128)S(1)}, s32[]{:T(128)}, f32[4,1,8,128,128]{4,3,2,0,1:T(8,128)}, f32[4,1,8,128,128]{4,3,2,0,1:T(8,1...) while((s32[]{:T(128)}, f32[1,8,128,128]{2,3,1,0:T(8,128)S(1)}, s32[]{:T(128)}, ...), condition=%wide.region_11.14_spmd.clone, body=%wide.region_10.13_spmd.clone.sunk | while | flops 201850880 | bytes 5769377 | solution.py:28
  423.0 2.1 fusion.454
  426.4 2.1 fusion.454
  429.9 2.1 fusion.454
  433.3 2.1 fusion.454
  438.5 221.0 %while.135 = (s32[]{:T(128)}, f32[1,8,128,128]{3,2,1,0:T(8,128)S(1)}, f32[2,1,8,64,128]{4,3,0,2,1:T(8,128)}, f32[2,1,8,64,128]{4,3,0,2,1:T(8,128)}, bf16[2,1,8,6...) while((s32[]{:T(128)}, ...), condition=%wide.region_23.26_spmd.clone.clone, body=%wide.region_12.25_spmd.clone.clone.sunk | while | flops 1034926144 | bytes 37745968 | solution.py:86
  447.4 2.2 convolution_bitcast_fusion.23
  449.5 1.4 fusion.418
  452.9 40.0 %custom-call.55 = f32[8,1,64,64]{2,3,1,0:T(8,128)} custom-call(f32[8,1,64,64]{3,2,1,0:T(8,128)S(1)} %add_bitcast_fusion.3), custom_call_target="InvertDiagBlocksLowerTriangular" | custom-call | tf_op jit(solution)/shard_map/transpose(jvp())/while/body/eval_jaxpr/jit(_solve_triangular)/vmap()/triangular_solve | solution.py:66
  492.9 2.0 fusion.428
  496.1 40.0 %custom-call.54 = f32[8,1,64,64]{2,3,1,0:T(8,128)} custom-call(f32[8,1,64,64]{3,2,1,0:T(8,128)S(1)} %fusion.420), custom_call_target="InvertDiagBlocksLowerTriangular" | custom-call | tf_op jit(solution)/shard_map/transpose(jvp())/while/body/eval_jaxpr/jit(_solve_triangular)/vmap()/triangular_solve/custom-call.0 | solution.py:66
  536.0 2.1 bitcast_dynamic-update-slice_fusion.27
  538.1 1.3 fusion.432
  539.4 1.3 fusion.429
  544.0 1.5 convolution_bitcast_fusion.25
  545.5 1.5 convolution_bitcast_fusion.26
  547.1 1.6 fusion.430
  553.4 2.1 convolution_bitcast_fusion.23
  555.6 1.4 fusion.418
  559.0 40.0 %custom-call.55 = f32[8,1,64,64]{2,3,1,0:T(8,128)} custom-call(f32[8,1,64,64]{3,2,1,0:T(8,128)S(1)} %add_bitcast_fusion.3), custom_call_target="InvertDiagBlocksLowerTriangular" | custom-call | tf_op jit(solution)/shard_map/transpose(jvp())/while/body/eval_jaxpr/jit(_solve_triangular)/vmap()/triangular_solve | solution.py:66
  598.9 2.0 fusion.428
  602.1 40.0 %custom-call.54 = f32[8,1,64,64]{2,3,1,0:T(8,128)} custom-call(f32[8,1,64,64]{3,2,1,0:T(8,128)S(1)} %fusion.420), custom_call_target="InvertDiagBlocksLowerTriangular" | custom-call | tf_op jit(solution)/shard_map/transpose(jvp())/while/body/eval_jaxpr/jit(_solve_triangular)/vmap()/triangular_solve/custom-call.0 | solution.py:66
  642.1 2.0 bitcast_dynamic-update-slice_fusion.27
  644.1 1.3 fusion.432
  645.5 1.3 fusion.429
  650.1 1.5 convolution_bitcast_fusion.25
  651.5 1.5 convolution_bitcast_fusion.26
  653.1 1.6 fusion.430
  659.5 1.3 copy.223
  662.9 1.3 copy.220
  (463 shorter events, 99.1 us)
Async XLA Ops:
  7.2 351.7 %copy-start = (bf16[8,128,128]{2,1,0:T(8,128)(2,1)S(1)}, bf16[8,128,128]{2,1,0:T(8,128)(2,1)}, u32[]{:S(2)}) copy-start(bf16[8,128,128]{2,1,0:T(8,128)(2,1)} %param.39) | copy-start | bytes 786436
  7.2 14.1 %copy-start.46 = (bf16[1,128,1024]{2,1,0:T(8,128)(2,1)S(1)}, bf16[1,128,1024]{2,1,0:T(8,128)(2,1)}, u32[]{:S(2)}) copy-start(bf16[1,128,1024]{2,1,0:T(8,128)(2,1)} %param.28) | copy-start | bytes 786436
  7.2 151.5 %reduce-scatter.3.cloned.1.call-start = ((), (), s32[]{:S(2)}) async-start(), calls=%async_computation.4 | async-start | bytes 786432 | tf_op jit(solution)/shard_map/reduce_scatter | solution.py:253
  8.3 12.9 %copy-start.37 = (bf16[1,128,512]{1,2,0:T(8,128)(2,1)}, bf16[1,128,512]{1,2,0:T(8,128)(2,1)S(1)}, u32[]{:S(2)}) copy-start(bf16[1,128,512]{1,2,0:T(8,128)(2,1)S(1)} %copy.233) | copy-start | bytes 393220
  9.4 11.8 %copy-start.39 = (bf16[1,128,512]{1,2,0:T(8,128)(2,1)}, bf16[1,128,512]{1,2,0:T(8,128)(2,1)S(1)}, u32[]{:S(2)}) copy-start(bf16[1,128,512]{1,2,0:T(8,128)(2,1)S(1)} %copy.234) | copy-start | bytes 393220
  10.2 138.6 %collective-permute-start = (bf16[2,1,128,512]{2,3,1,0:T(8,128)(2,1)}, bf16[2,1,128,512]{2,3,1,0:T(8,128)(2,1)}, u32[]{:S(2)}, u32[]{:S(2)}) collective-permute-start(bf16[2,1,128,512]{2,3,1,0:T(8,128)(2,1)} %pad_maximum_fusion.1), channel_id=1, source_target_pairs={{0,8},{4,12},{1,9},{5,13},{2,10},{6,14},{3,11},{7,15},{16,24},{20,... | collective-permute-start | bytes 786440 | tf_op jit(solution)/shard_map/ppermute | solution.py:34
  16.8 132.0 %collective-permute-start.1 = (bf16[2,1,128,512]{2,3,1,0:T(8,128)(2,1)}, bf16[2,1,128,512]{2,3,1,0:T(8,128)(2,1)}, u32[]{:S(2)}, u32[]{:S(2)}) collective-permute-start(bf16[2,1,128,512]{2,3,1,0:T(8,128)(2,1)} %pad_maximum_fusion.1), channel_id=1, source_target_pairs={{0,4},{4,8},{8,12},{1,5},{5,9},{9,13},{2,6},{6,10},{10,14},{3,7},{... | collective-permute-start | bytes 786440 | tf_op jit(solution)/shard_map/ppermute | solution.py:34
  21.1 4.5 copy-start.29
  23.4 2.9 copy-start.62
  23.4 3.0 copy-start.63
  23.4 3.1 copy-start.48
  25.6 3.8 copy-start.1
  73.9 3.3 copy-start.7
  73.9 3.3 copy-start.22
  73.9 3.3 copy-start.26
  74.1 3.8 copy-start.24
  81.2 4.0 copy-start.66
  130.3 3.3 copy-start.7
  130.3 3.3 copy-start.22
  130.3 3.3 copy-start.26
  130.6 3.8 copy-start.24
  137.6 4.0 copy-start.66
  142.2 3.6 copy-start.3
  142.2 3.6 copy-start.64
  142.2 3.7 copy-start.49
  143.4 3.3 copy-start.33
  145.8 3.0 copy-start.38
  145.8 3.0 copy-start.40
  145.8 29.8 %reduce-scatter.5.cloned.1.call-start = ((), (), s32[]{:S(2)}) async-start(), calls=%async_computation.5 | async-start | bytes 786432 | tf_op jit(solution)/shard_map/reduce_scatter | solution.py:254
  154.5 21.4 %copy-start.10 = (f32[2,1,8,64,64]{3,4,2,1,0:T(8,128)S(1)}, f32[2,1,8,64,64]{3,4,2,1,0:T(8,128)}, u32[]{:S(2)}) copy-start(f32[2,1,8,64,64]{3,4,2,1,0:T(8,128)} %get-tuple-element.3524) | copy-start | bytes 786436
  154.5 21.5 %copy-start.68 = (f32[2,1,8,1,1]{2,4,3,1,0:T(1,128)S(1)}, f32[2,1,8,1,1]{2,4,3,1,0:T(1,128)}, u32[]{:S(2)}) copy-start(f32[2,1,8,1,1]{2,4,3,1,0:T(1,128)} %get-tuple-element.3517) | copy-start | bytes 196
  154.5 263.7 %all-reduce.4.cloned.1.call-start = ((), (), s32[]{:S(2)}) async-start(), calls=%async_computation.6 | async-start | bytes 1048576 | tf_op jit(solution)/shard_map/psum | solution.py:251
  175.7 244.3 %all-gather.7.cloned.1.call-start = ((), (), s32[]{:S(2)}) async-start(), calls=%async_computation.3 | async-start | bytes 2621440 | tf_op jit(solution)/shard_map/all_gather | solution.py:17
  270.6 151.0 %all-gather.5.cloned.1.call-start = ((), (), s32[]{:S(2)}) async-start(), calls=%async_computation.2 | async-start | bytes 2621440 | tf_op jit(solution)/shard_map/all_gather | solution.py:17
  366.1 21.5 %collective-permute-start.2 = (bf16[2,1,128,512]{3,2,1,0:T(8,128)(2,1)}, bf16[2,1,128,512]{3,2,1,0:T(8,128)(2,1)}, u32[]{:S(2)}, u32[]{:S(2)}) collective-permute-start(bf16[2,1,128,512]{3,2,1,0:T(8,128)(2,1)} %get-tuple-element.2675), channel_id=1, source_target_pairs={{4,0},{8,4},{12,8},{5,1},{9,5},{13,9},{6,2},{10,6},{14,10},{7,3},{... | collective-permute-start | bytes 786440 | tf_op jit(solution)/shard_map/ppermute | solution.py:34
  367.4 49.0 %collective-permute-start.3 = (bf16[2,1,128,512]{3,2,1,0:T(8,128)(2,1)}, bf16[2,1,128,512]{3,2,1,0:T(8,128)(2,1)}, u32[]{:S(2)}, u32[]{:S(2)}) collective-permute-start(bf16[2,1,128,512]{3,2,1,0:T(8,128)(2,1)} %get-tuple-element.2676), channel_id=1, source_target_pairs={{8,0},{12,4},{9,1},{13,5},{10,2},{14,6},{11,3},{15,7},{24,16},{28,... | collective-permute-start | bytes 786440 | tf_op jit(solution)/shard_map/ppermute | solution.py:34
  438.5 222.3 %copy-start.61 = (f32[8,128]{1,0:T(8,128)S(1)}, f32[8,128]{1,0:T(8,128)}, u32[]{:S(2)}) copy-start(f32[8,128]{1,0:T(8,128)} %get-tuple-element.2683) | copy-start | bytes 12292
  447.4 3.6 copy-start.28
  447.4 4.8 copy-start.15
  449.5 3.3 copy-start.5
  536.0 3.4 copy-start.16
  538.1 4.2 copy-start.65
  539.4 4.5 copy-start.52
  539.4 4.5 copy-start.55
  543.9 3.1 copy-start.6
  543.9 4.7 copy-start.53
  544.0 4.7 copy-start.56
  544.0 4.7 copy-start.4
  544.0 4.7 copy-start.35
  553.4 3.6 copy-start.28
  553.4 4.8 copy-start.15
  555.6 3.3 copy-start.5
  642.1 3.4 copy-start.16
  644.1 4.2 copy-start.65
  645.5 4.5 copy-start.52
  645.5 4.5 copy-start.55
  650.0 3.1 copy-start.6
  650.0 4.7 copy-start.53
  650.0 4.7 copy-start.56
  650.0 4.7 copy-start.4
  650.0 4.7 copy-start.35
  660.8 3.4 copy-start.19
  660.8 3.4 copy-start.60
  664.2 3.5 copy-start.50
  (43 other events, 71.2 us)
Sparse Core Ops, SparseCore 0:
  145.9 12.7 reduce-scatter.2
  161.0 14.5 reduce-scatter.4
  178.0 39.9 all-reduce.3
  270.7 46.5 all-gather.6
  359.0 62.6 all-gather.4
where the time goes:
time: 681 us; the launch traced here: 675 us
  other arithmetic  431 us (63%)
  matrix products  94.3 us (14%)
  waiting for transfers between devices  66.1 us (10%)
  local copies, waits for them, and re-layouts  44.2 us (6%)
  between operations  14.9 us (2%)
  starting transfers between devices  13.8 us (2%)
  loops' own time  10.5 us (2%)
    another operation x38, other arithmetic, advance(): jax.scipy.linalg.solve_triangular(identity + lower_part, target, lower=Tr...  406 us
    ppermute x4, waiting for transfers between devices, from_behind(): return lax.ppermute(x, axis, pairs)  43.6 us
    reduce_scatter x1, waiting for transfers between devices, body(): lax.psum_scatter(totals[1], 'dp', scatter_dimension=1, tiled=True)  16.9 us
    dot_general x10, matrix products, advance(): jnp.einsum('bhsv,bhsk->bhvk', written, carried_keys, precision=HIGHEST_PR...  15.9 us
    unnamed x102, local copies, waits for them, and re-layouts  15.3 us
    dot_general x10, matrix products, advance(): jnp.einsum('bhtk,bhvk->bhtv', key_part, state_now, precision=HIGHEST_PREC...  14 us
  transfers between devices with their start and end apart: 9, of which 5 were waited for; matrix products, arithmetic and copies ran while one was open for 48% of the time, Pallas kernels for 0%

commit v1 on v0

v1 whole, which is shorter than its diff:
```python
import functools

import jax
import jax.numpy as jnp
from jax import lax
from jax.experimental import pallas as pl
from jax.experimental.pallas import tpu as pltpu
from jax.sharding import PartitionSpec as P

WINDOW = 256
NORM_EPSILON = 1e-06
MASK_FLOOR = -1e30
F32 = jnp.float32
BF16 = jnp.bfloat16
NN = ((1,), (0,))
NT = ((1,), (1,))
TN = ((0,), (0,))
INVERSE_PASSES = 3
PASSES = 3


def dot(a, b, dims):
    return lax.dot_general(a, b, (dims, ((), ())), preferred_element_type=F32)


def parts_of(a, passes):
    if a.dtype == BF16:
        return (a,)
    high = a.astype(BF16)
    if passes == 1:
        return (high,)
    return (high, (a - high.astype(F32)).astype(BF16))


def mm(a, b, dims, passes=None):
    passes = PASSES if passes is None else passes
    left, right = parts_of(a, passes), parts_of(b, passes)
    total = dot(left[0], right[0], dims)
    if len(left) > 1:
        total = total + dot(left[1], right[0], dims)
    if len(right) > 1:
        total = total + dot(left[0], right[1], dims)
    return total


def lockstep(steps):
    steps = list(steps)
    while steps:
        alive = []
        for step in steps:
            try:
                next(step)
                alive.append(step)
            except StopIteration:
                pass
        steps = alive


def token_facts(q, k, gate, beta):
    rows = q.shape[0]
    t = lax.broadcasted_iota(jnp.int32, (rows, rows), 0)
    s = lax.broadcasted_iota(jnp.int32, (rows, rows), 1)
    eye, within, strict = t == s, t >= s, t > s
    pick = lambda mask, x, axis: jnp.sum(jnp.where(mask, x, 0.0), axis=axis, keepdims=True)
    gate_col = pick(eye, gate, 1)
    beta_col = pick(eye, beta, 1)
    sum_col = pick(within, gate, 1)
    sum_row = pick(t <= s, gate_col, 0)
    last = sum_col[rows - 1 : rows]
    ratios = jnp.where(within, jnp.exp(jnp.where(within, sum_col - sum_row, 0.0)), 0.0)
    qf, kf = q.astype(F32), k.astype(F32)
    rq = 1.0 / jnp.sqrt(jnp.sum(qf * qf, axis=1, keepdims=True) + NORM_EPSILON)
    rk = 1.0 / jnp.sqrt(jnp.sum(kf * kf, axis=1, keepdims=True) + NORM_EPSILON)
    rk_row = pick(eye, rk, 0)
    kk = dot(k, k, NT) * (rk * rk_row)
    qk = dot(q, k, NT) * (rq * rk_row)
    return dict(
        t=t, s=s, eye=eye, within=within, strict=strict, pick=pick, beta=beta_col,
        decay=jnp.exp(sum_col), last=last, tail=jnp.exp(last - sum_col), ratios=ratios,
        rq=rq, rk=rk, qn=qf * rq, kn=kf * rk, kk=kk, qk=qk,
    )


def ahead_kernel(per, q_ref, k_ref, v_ref, cot_ref, gate_ref, beta_ref, state_ref, rot_ref,
                 local_ref, move_ref, w_ref, y_ref, z_ref, ks_ref, qs_ref, grad_ref, term_ref):
    first = pl.program_id(1) * per

    def head(i):
        lanes = slice(i * 128, (i + 1) * 128)
        q, k, v, cot = (r[0, :, lanes] for r in (q_ref, k_ref, v_ref, cot_ref))
        gate = gate_ref[0, pl.ds(first + i, 1), :]
        beta = beta_ref[0, pl.ds(first + i, 1), :]
        out_grad = dot(cot, rot_ref[i], NN).astype(BF16)
        grad_ref[0, i] = out_grad
        f = token_facts(q, k, gate, beta)
        yield
        state = state_ref[0, 0, i]
        seen_k = mm(k, state, NT) * f["rk"]
        seen_q = mm(q, state, NT) * f["rq"]
        ks_ref[0, i] = seen_k
        qs_ref[0, i] = seen_q
        lower = jnp.where(f["strict"], f["beta"] * f["ratios"] * f["kk"], 0.0)
        t, s = f["t"], f["s"]
        rows = q.shape[0]
        inverse = jnp.where(f["eye"], 1.0, 0.0)
        size = 1
        while size < rows:
            mask = (t // (2 * size) == s // (2 * size)) & (t // size != s // size)
            part = jnp.where(mask, lower, 0.0)
            if size == 1:
                inverse = inverse - part
            else:
                half = mm(part, inverse, NN, INVERSE_PASSES)
                yield
                inverse = inverse - mm(inverse, half, NN, INVERSE_PASSES)
                yield
            size *= 2
        bd = f["beta"] * f["decay"]
        x = mm(inverse, bd * f["kn"], NN)
        w = mm(inverse, f["beta"] * v.astype(F32) - bd * seen_k, NN)
        probs = f["ratios"] * f["qk"]
        tail_k = f["tail"] * f["kn"]
        yield
        w_ref[0, i] = w
        seen = mm(probs, out_grad, TN)
        z = mm(inverse, tail_k, TN)
        z_ref[0, i] = z
        out = f["decay"] * seen_q + mm(probs, w, NN)
        term_ref[i] = dot(cot, out.astype(BF16), TN)
        yield
        y = mm(inverse, seen, TN)
        y_ref[0, i] = y
        keep = jnp.exp(f["last"])
        move_ref[0, i] = jnp.where(f["eye"], keep, 0.0) - mm(tail_k, x, TN)
        yield
        og = f["decay"] * out_grad.astype(F32)
        local_ref[0, i] = mm(og, f["qn"], TN) - mm(bd * y, f["kn"], TN)

    lockstep(head(i) for i in range(per))


def back_kernel(per, q_ref, k_ref, v_ref, gate_ref, beta_ref, state_ref,
                later_ref, w_ref, y_ref, z_ref, ks_ref, qs_ref, grad_ref,
                dq_ref, dk_ref, dv_ref, dgate_ref, dbeta_ref):
    first = pl.program_id(1) * per

    def head(i):
        lanes = slice(i * 128, (i + 1) * 128)
        q, k, v = (r[0, :, lanes] for r in (q_ref, k_ref, v_ref))
        at = pl.ds(first + i, 1)
        f = token_facts(q, k, gate_ref[0, at, :], beta_ref[0, at, :])
        later = later_ref[0, i]
        state = state_ref[0, 0, i]
        w, seen_k, seen_q, out_grad = w_ref[0, i], ks_ref[0, i], qs_ref[0, i], grad_ref[0, i]
        pick, eye, within, strict = f["pick"], f["eye"], f["within"], f["strict"]
        total = lambda x: jnp.sum(x, axis=1, keepdims=True)
        dr = y_ref[0, i] + mm(z_ref[0, i], later, NT)
        wh = f["tail"] * mm(w, later, NN)
        dp = jnp.where(within, mm(out_grad, w, NT), 0.0)
        yield
        da = jnp.where(strict, -mm(dr, w, NT), 0.0)
        og = f["decay"] * out_grad.astype(F32)
        dks = -(f["beta"] * f["decay"]) * dr
        yield
        dqk = dp * f["ratios"]
        dar = da * f["ratios"]
        dkk = f["beta"] * dar
        dark = dar * f["kk"]
        e = f["beta"] * dark + dqk * f["qk"]
        dkn = mm(dks, state, NN) + mm(dkk, f["kn"], NN) + wh
        dqn = mm(og, state, NN) + mm(dqk, f["kn"], NN)
        yield
        dkn = dkn + mm(dkk, f["kn"], TN) + mm(dqk, f["qn"], TN)
        yield
        vf = v.astype(F32)
        dbeta = total(dark) + total(dr * (vf - f["decay"] * seen_k))
        carried = total(f["kn"] * wh)
        dsum = total(e) + total(og * seen_q + dks * seen_k) - carried
        dsum = dsum - pick(eye, jnp.sum(e, axis=0, keepdims=True), 1)
        end = jnp.sum(carried, axis=0, keepdims=True) + jnp.exp(f["last"]) * jnp.sum(
            total(later * state), axis=0, keepdims=True
        )
        dgate_ref[0, at, :] = pick(within, dsum, 0) + end
        dbeta_ref[0, at, :] = pick(eye, dbeta, 0)
        dv_ref[0, :, lanes] = (f["beta"] * dr).astype(BF16)
        dq_ref[0, :, lanes] = (f["rq"] * (dqn - f["qn"] * total(f["qn"] * dqn))).astype(BF16)
        dk_ref[0, :, lanes] = (f["rk"] * (dkn - f["kn"] * total(f["kn"] * dkn))).astype(BF16)

    lockstep(head(i) for i in range(per))


def window_kernel(reach, group, place_ref, q_ref, cot_ref, rot_ref, *refs):
    keys = jnp.concatenate([r[0] for r in refs[: reach + 1]], axis=0)
    values = jnp.concatenate([r[0] for r in refs[reach + 1 : 2 * reach + 2]], axis=0)
    dq_ref, term_ref = refs[2 * reach + 2 : 2 * reach + 4]
    key_outs = refs[2 * reach + 4 : 3 * reach + 5]
    value_outs = refs[3 * reach + 5 :]
    rows = q_ref.shape[1]
    scale = 128 ** (-0.5)
    t = lax.broadcasted_iota(jnp.int32, (rows, keys.shape[0]), 0)
    u = lax.broadcasted_iota(jnp.int32, (rows, keys.shape[0]), 1) - reach * rows
    allowed = (u <= t) & (u > t - WINDOW) & (u + place_ref[0, 0] * rows >= 0)
    key_sum, value_sum = [], []

    def head(g):
        lanes = slice(g * 128, (g + 1) * 128)
        q, cot = q_ref[0, :, lanes], cot_ref[0, :, lanes]
        out_grad = dot(cot, rot_ref[g], NN).astype(BF16)
        scores = jnp.where(allowed, scale * dot(q, keys, NT), MASK_FLOOR)
        yield
        prob_grad = dot(out_grad, values, NT)
        weights = jnp.exp(scores - jnp.max(scores, axis=1, keepdims=True))
        probs = weights / jnp.sum(weights, axis=1, keepdims=True)
        low = probs.astype(BF16)
        yield
        out = dot(low, values, NN)
        row_dot = jnp.sum(probs * prob_grad, axis=1, keepdims=True)
        dscore = (probs * (prob_grad - row_dot)).astype(BF16)
        yield
        dq_ref[0, :, lanes] = (scale * dot(dscore, keys, NN)).astype(BF16)
        key_sum.append(dot(dscore, q, TN))
        value_sum.append(dot(low, out_grad, TN))
        term_ref[g] = dot(cot, out.astype(BF16), TN)

    lockstep(head(g) for g in range(group))
    key_term = (scale * functools.reduce(jnp.add, key_sum)).astype(BF16)
    value_term = functools.reduce(jnp.add, value_sum).astype(BF16)
    for j in range(reach + 1):
        key_outs[j][0] = key_term[j * rows : (j + 1) * rows]
        value_outs[j][0] = value_term[j * rows : (j + 1) * rows]


def per_head(shape, per):
    return pl.BlockSpec((1, per) + shape, lambda b, h: (b, h, 0, 0))


def shifted(x, by):
    size = lax.axis_size("seq")
    return lax.ppermute(x, "seq", [(i, i + by) for i in range(size) if 0 <= i + by < size])


def body(gdn_query, gdn_key, gdn_value, gdn_cot, gate_log, beta, state_in, gdn_rot,
         att_query, att_key, att_value, att_cot, att_rot):
    rows_s, tokens, width = gdn_query.shape
    heads = gdn_rot.shape[0]
    n_seq = lax.axis_size("seq")
    kv_width = att_key.shape[2]
    kv_count = kv_width // 128
    group = heads // kv_count
    reach = -(-WINDOW // tokens)
    per = 4
    params = pltpu.CompilerParams(vmem_limit_bytes=48 * 2**20)
    flops = 2 * heads * 128**3

    keys = [shifted(att_key, d) for d in range(reach, 0, -1)] + [att_key]
    values = [shifted(att_value, d) for d in range(reach, 0, -1)] + [att_value]

    tok = pl.BlockSpec((1, tokens, per * 128), lambda b, h: (b, 0, h))
    gate_spec = pl.BlockSpec((1, heads, tokens), lambda b, h: (b, 0, 0))
    state_spec = pl.BlockSpec((1, 1, per, 128, 128), lambda b, h: (b, 0, h, 0, 0))
    rot_spec = pl.BlockSpec((per, 128, 128), lambda b, h: (h, 0, 0))
    square, token_wide = per_head((128, 128), per), per_head((tokens, 128), per)
    like = lambda *shape, dtype=F32: jax.ShapeDtypeStruct(shape, dtype)
    wide = like(rows_s, heads, tokens, 128)
    mat = like(rows_s, heads, 128, 128)

    local, move, w, y, z, ks, qs, grad, gdn_term = pl.pallas_call(
        functools.partial(ahead_kernel, per),
        name="ahead",
        grid=(rows_s, heads // per),
        in_specs=[tok] * 4 + [gate_spec] * 2 + [state_spec, rot_spec],
        out_specs=[square] * 2 + [token_wide] * 6 + [rot_spec],
        out_shape=[mat, mat, wide, wide, wide, wide, wide,
                   like(rows_s, heads, tokens, 128, dtype=BF16), like(heads, 128, 128)],
        compiler_params=params,
        cost_estimate=pl.CostEstimate(flops=80 * flops, bytes_accessed=6 * 2**20, transcendentals=0),
    )(gdn_query, gdn_key, gdn_value, gdn_cot, gate_log, beta, state_in, gdn_rot)

    travel = BF16 if n_seq <= 8 else F32
    later = shifted(local.astype(travel), -1)
    for _ in range(n_seq - 2):
        carried = local + jnp.einsum(
            "bhvk,bhkl->bhvl", later.astype(F32), move, precision=lax.Precision.HIGH
        )
        later = shifted(carried.astype(travel), -1)
    later = later.astype(F32)

    q_spec = pl.BlockSpec((1, tokens, group * 128), lambda b, h: (b, 0, h))
    kv_spec = pl.BlockSpec((1, tokens, 128), lambda b, h: (b, 0, h))
    group_spec = pl.BlockSpec((group, 128, 128), lambda b, h: (h, 0, 0))
    kv_out = like(rows_s, tokens, kv_width, dtype=BF16)
    place = jnp.full((1, 1), lax.axis_index("seq"), jnp.int32)
    outs = pl.pallas_call(
        functools.partial(window_kernel, reach, group),
        name="window",
        grid=(rows_s, kv_count),
        in_specs=[pl.BlockSpec(memory_space=pltpu.SMEM), q_spec, q_spec, group_spec]
        + [kv_spec] * (2 * reach + 2),
        out_specs=[q_spec, group_spec] + [kv_spec] * (2 * reach + 2),
        out_shape=[like(rows_s, tokens, width, dtype=BF16), like(heads, 128, 128)]
        + [kv_out] * (2 * reach + 2),
        compiler_params=params,
        cost_estimate=pl.CostEstimate(flops=60 * flops, bytes_accessed=4 * 2**20, transcendentals=0),
    )(place, att_query, att_cot, att_rot, *keys, *values)
    att_dq, att_term = outs[:2]
    key_terms, value_terms = outs[2 : reach + 3], outs[reach + 3 :]
    dk, dv = key_terms[reach].astype(F32), value_terms[reach].astype(F32)
    for d in range(1, reach + 1):
        dk = dk + shifted(key_terms[reach - d], -d).astype(F32)
        dv = dv + shifted(value_terms[reach - d], -d).astype(F32)

    both = jnp.concatenate([gdn_term, att_term], axis=0)
    share = lax.psum(lax.psum_scatter(both, "dp", scatter_dimension=1, tiled=True), "seq")

    dq_spec = like(rows_s, tokens, width, dtype=BF16)
    gates = like(rows_s, heads, tokens)
    gdn_dq, gdn_dk, gdn_dv, dgate, dbeta = pl.pallas_call(
        functools.partial(back_kernel, per),
        name="back",
        grid=(rows_s, heads // per),
        in_specs=[tok] * 3 + [gate_spec] * 2 + [state_spec, square] + [token_wide] * 6,
        out_specs=[tok] * 3 + [gate_spec] * 2,
        out_shape=[dq_spec] * 3 + [gates] * 2,
        compiler_params=params,
        cost_estimate=pl.CostEstimate(flops=60 * flops, bytes_accessed=6 * 2**20, transcendentals=0),
    )(gdn_query, gdn_key, gdn_value, gate_log, beta, state_in, later, w, y, z, ks, qs, grad)

    return (gdn_dq, gdn_dk, gdn_dv, dgate, dbeta, share[:heads],
            att_dq, dk.astype(BF16), dv.astype(BF16), share[heads:])


def solution(mesh):
    tokens = P(("group", "dp"), "seq", "head")
    gates = P(("group", "dp"), "head", "seq")
    rot = P("head", None, None)
    rot_grad = P(("group", "head"), "dp", None)
    return jax.shard_map(
        body,
        mesh=mesh,
        in_specs=(tokens,) * 4
        + (gates,) * 2
        + (P(("group", "dp"), "seq", "head", None, None), rot)
        + (tokens,) * 4
        + (rot,),
        out_specs=(tokens,) * 3 + (gates,) * 2 + (rot_grad,) + (tokens,) * 3 + (rot_grad,),
        check_vma=False,
    )
```

time: 681 us -> 121 us (0.18)
  other arithmetic: 431 us -> 4.57 us
  matrix products: 94.3 us -> 1.33 us
  local copies, waits for them, and re-layouts: 44.2 us -> 11.7 us
  Pallas kernels: 0 us -> 20.6 us
  waiting for transfers between devices: 66.1 us -> 45.8 us
  loops' own time: 10.5 us -> 0 us
  starting transfers between devices: 13.8 us -> 21.8 us
    another operation x66 -> x0, other arithmetic: 411 us -> none  [the longest x38 406 us: advance(): jax.scipy.linalg.solve_triangular(identity + lower_part, target, lower=Tr...]
    dot_general x65 -> x2, matrix products: 82.6 us -> 1.33 us  [body(): jnp.einsum('bhvk,bhkl->bhvl', later.astype(F32), move, precision=lax.Prec...]
    reduce_scatter x2 -> x1, waiting for transfers between devices: 20.7 us -> 0.02 us  [body(): lax.psum_scatter(both, 'dp', scatter_dimension=1, tiled=True)]
    pallas_call x0 -> x3, Pallas kernels: none -> 20.6 us  [the longest x1 10.2 us: body(): pl.pallas_call(functools.partial(ahead_kernel, per), name='ahead', grid=(...]
    psum x1, waiting for transfers between devices: 0.01 us -> 13.6 us  [body(): lax.psum(lax.psum_scatter(both, 'dp', scatter_dimension=1, tiled=True), '...]
    another operation x10 -> x0, matrix products: 11.7 us -> none  [advance(): jax.scipy.linalg.solve_triangular(identity + lower_part, target, lower=Tr...]
    ppermute x4 -> x11, waiting for transfers between devices: 43.6 us -> 32.1 us  [shifted(): lax.ppermute(x, 'seq', [(i, i + by) for i in range(size) if 0 <= i + by <...]
    another operation x5 -> x0, loops' own time: 10.5 us -> none  [the longest x4 10.3 us: stretch_delta(): final_state, outputs = lax.scan(advance, start_state, members)]
  transfers between devices with their start and end apart: 9 -> 13, of which waited for: 5 -> 5; matrix products, arithmetic and copies ran while one was open for 48% -> 4% of each run, Pallas kernels for 0% -> 13%
where the time goes in v1:
time: 121 us; the launch traced here: 120 us
  waiting for transfers between devices  45.8 us (38%)
  starting transfers between devices  21.8 us (18%)
  Pallas kernels  20.6 us (17%)
  between operations  14.4 us (12%)
  local copies, waits for them, and re-layouts  11.7 us (10%)
  other arithmetic  4.57 us (4%)
  matrix products  1.33 us (1%)
    ppermute x11, waiting for transfers between devices, shifted(): lax.ppermute(x, 'seq', [(i, i + by) for i in range(size) if 0 <= i + by <...  32.1 us
    ppermute x11, starting transfers between devices, shifted(): lax.ppermute(x, 'seq', [(i, i + by) for i in range(size) if 0 <= i + by <...  21.7 us
    psum x1, waiting for transfers between devices, body(): lax.psum(lax.psum_scatter(both, 'dp', scatter_dimension=1, tiled=True), '...  13.6 us
    pallas_call x1, Pallas kernels, body(): pl.pallas_call(functools.partial(ahead_kernel, per), name='ahead', grid=(...  10.2 us
    unnamed x50, local copies, waits for them, and re-layouts  9.82 us
    pallas_call x1, Pallas kernels, body(): pl.pallas_call(functools.partial(back_kernel, per), name='back', grid=(ro...  5.56 us
    pallas_call x1, Pallas kernels, body(): pl.pallas_call(functools.partial(window_kernel, reach, group), name='wind...  4.83 us
  transfers between devices with their start and end apart: 13, of which 5 were waited for; matrix products, arithmetic and copies ran while one was open for 4% of the time, Pallas kernels for 13%

profile of v1, /device:TPU:0, one launch (start us, length us, event | category | flops | bytes accessed | tf_op | source)
XLA Modules:
  0.0 120.0 jit_solution(6470045691904228785)
XLA Ops:
  7.2 0.0 copy-start.14
  7.2 0.0 reduce-scatter.2.cloned.1.call-start
  7.2 5.9 %collective-permute-start.3 = (bf16[1,128,512]{2,1,0:T(8,128)(2,1)}, bf16[1,128,512]{2,1,0:T(8,128)(2,1)S(1)}, u32[]{:S(2)}, u32[]{:S(2)}) collective-permute-start(bf16[1,128,512]{2,1,0:T(8,128)(2,1)} %refs_2_.1), channel_id=1, source_target_pairs={{0,8},{4,12},{1,9},{5,13},{2,10},{6,14},{3,11},{7,15},{16,24},{20,... | collective-permute-start | bytes 393224 | tf_op jit(solution)/shard_map/ppermute | solution.py:239
  13.2 3.5 %collective-permute-start.4 = (bf16[1,128,512]{2,1,0:T(8,128)(2,1)}, bf16[1,128,512]{2,1,0:T(8,128)(2,1)S(1)}, u32[]{:S(2)}, u32[]{:S(2)}) collective-permute-start(bf16[1,128,512]{2,1,0:T(8,128)(2,1)} %refs_2_.1), channel_id=1, source_target_pairs={{0,4},{4,8},{8,12},{1,5},{5,9},{9,13},{2,6},{6,10},{10,14},{3,7},{... | collective-permute-start | bytes 393224 | tf_op jit(solution)/shard_map/ppermute | solution.py:239
  16.7 1.3 %collective-permute-start.5 = (bf16[1,128,512]{2,1,0:T(8,128)(2,1)}, bf16[1,128,512]{2,1,0:T(8,128)(2,1)S(1)}, u32[]{:S(2)}, u32[]{:S(2)}) collective-permute-start(bf16[1,128,512]{2,1,0:T(8,128)(2,1)} %refs_5_.1), channel_id=1, source_target_pairs={{0,8},{4,12},{1,9},{5,13},{2,10},{6,14},{3,11},{7,15},{16,24},{20,... | collective-permute-start | bytes 393224 | tf_op jit(solution)/shard_map/ppermute | solution.py:239
  18.0 1.9 %collective-permute-start.6 = (bf16[1,128,512]{2,1,0:T(8,128)(2,1)}, bf16[1,128,512]{2,1,0:T(8,128)(2,1)S(1)}, u32[]{:S(2)}, u32[]{:S(2)}) collective-permute-start(bf16[1,128,512]{2,1,0:T(8,128)(2,1)} %refs_5_.1), channel_id=1, source_target_pairs={{0,4},{4,8},{8,12},{1,5},{5,9},{9,13},{2,6},{6,10},{10,14},{3,7},{... | collective-permute-start | bytes 393224 | tf_op jit(solution)/shard_map/ppermute | solution.py:239
  19.9 0.0 copy-done.14
  19.9 0.0 copy-start.1
  19.9 0.9 copy-done.1
  20.9 0.9 copy-done.2
  21.8 0.9 copy-done.6
  22.8 0.9 copy-done.8
  23.7 0.9 copy-done.10
  24.7 0.7 copy-done.15
  25.4 0.0 copy-start.13
  25.4 10.2 %ahead.1 = (f32[1,8,128,128]{3,2,1,0:T(8,128)S(1)}, f32[1,8,128,128]{3,2,1,0:T(8,128)S(1)}, f32[1,8,128,128]{3,2,1,0:T(8,128)S(1)}, f32[1,8,128,128]{3,2,1,0:T(8...) custom-call(bf16[1,128,1024]{2,1,0:T(8,128)(2,1)S(1)} %copy-done.6, ...), custom_call_target="tpu_custom_call" | custom-call | flops 2684354560 | bytes 6291456 | tf_op jit(solution)/shard_map/ahead/pallas_call | solution.py:267
  35.6 0.0 copy-start.17
  35.6 0.8 copy-done.17
  36.4 0.8 copy-done.19
  37.2 0.7 copy-done.23
  37.9 0.0 collective-permute-done.3.refs_0_
  37.9 0.0 collective-permute-done.4.refs_1_
  37.9 0.0 collective-permute-done.5.refs_3_
  37.9 0.0 collective-permute-done.6.refs_4_
  37.9 0.0 copy-done.3
  37.9 0.0 copy-done.4
  37.9 0.0 copy-done.5
  37.9 0.0 copy-done.12
  37.9 4.8 %window.1 = (bf16[1,128,1024]{2,1,0:T(8,128)(2,1)}, f32[8,128,128]{2,1,0:T(8,128)S(1)}, bf16[1,128,512]{2,1,0:T(8,128)(2,1)S(1)}, bf16[1,128,512]{2,1,0:T(8,128)...) custom-call(s32[1,1]{1,0:T(1,128)} %bitcast.5.place_ref, ...), custom_call_target="tpu_custom_call" | custom-call | flops 2013265920 | bytes 4194304 | tf_op jit(solution)/shard_map/window/pallas_call | solution.py:293
  42.8 1.1 pad_maximum_fusion
  43.8 0.0 reduce-scatter.2.cloned.1.call-update
  43.9 0.0 all-reduce.2.cloned.1.call-start
  44.0 1.3 %collective-permute-start = (bf16[1,8,128,128]{3,2,1,0:T(8,128)(2,1)S(1)}, bf16[1,8,128,128]{3,2,1,0:T(8,128)(2,1)S(1)}, u32[]{:S(2)}, u32[]{:S(2)}) collective-permute-start(bf16[1,8,128,128]{3,2,1,0:T(8,128)(2,1)S(1)} %convert_element_type.38), channel_id=1, source_target_pairs={{4,0},{8,4},{12,8},{5,1},{9,5},{13,9},{6,2},{10,6},{14,10},{7,3},{... | collective-permute-start | bytes 786440 | tf_op jit(solution)/shard_map/ppermute | solution.py:239
  45.3 8.1 %collective-permute-done = bf16[1,8,128,128]{3,2,1,0:T(8,128)(2,1)S(1)} collective-permute-done((bf16[1,8,128,128]{3,2,1,0:T(8,128)(2,1)S(1)}, bf16[1,8,128,128]{3,2,1,0:T(8,128)(2,1)S(1)}, u32[]{:S(2)}, u32[]{:S(2)}) %collective-permute-start) | collective-permute-done | bytes 262176 | tf_op jit(solution)/shard_map/ppermute | solution.py:239
  53.4 0.3 fusion.3
  53.7 1.3 %collective-permute-start.1 = (bf16[1,8,128,128]{3,2,1,0:T(8,128)(2,1)S(1)}, bf16[1,8,128,128]{3,2,1,0:T(8,128)(2,1)S(1)}, u32[]{:S(2)}, u32[]{:S(2)}) collective-permute-start(bf16[1,8,128,128]{3,2,1,0:T(8,128)(2,1)S(1)} %fusion.3), channel_id=1, source_target_pairs={{4,0},{8,4},{12,8},{5,1},{9,5},{13,9},{6,2},{10,6},{14,10},{7,3},{... | collective-permute-start | bytes 786440 | tf_op jit(solution)/shard_map/ppermute | solution.py:239
  55.0 1.3 %collective-permute-start.10 = (bf16[1,128,512]{2,1,0:T(8,128)(2,1)S(1)}, bf16[1,128,512]{2,1,0:T(8,128)(2,1)}, u32[]{:S(2)}, u32[]{:S(2)}) collective-permute-start(bf16[1,128,512]{2,1,0:T(8,128)(2,1)S(1)} %get-tuple-element.53), channel_id=1, source_target_pairs={{8,0},{12,4},{9,1},{13,5},{10,2},{14,6},{11,3},{15,7},{24,16},{28,... | collective-permute-start | bytes 393224 | tf_op jit(solution)/shard_map/ppermute | solution.py:239
  56.3 1.3 %collective-permute-start.9 = (bf16[1,128,512]{2,1,0:T(8,128)(2,1)S(1)}, bf16[1,128,512]{2,1,0:T(8,128)(2,1)}, u32[]{:S(2)}, u32[]{:S(2)}) collective-permute-start(bf16[1,128,512]{2,1,0:T(8,128)(2,1)S(1)} %get-tuple-element.52), channel_id=1, source_target_pairs={{4,0},{8,4},{12,8},{5,1},{9,5},{13,9},{6,2},{10,6},{14,10},{7,3},{... | collective-permute-start | bytes 393224 | tf_op jit(solution)/shard_map/ppermute | solution.py:239
  57.6 1.3 %collective-permute-start.7 = (bf16[1,128,512]{2,1,0:T(8,128)(2,1)S(1)}, bf16[1,128,512]{2,1,0:T(8,128)(2,1)S(1)}, u32[]{:S(2)}, u32[]{:S(2)}) collective-permute-start(bf16[1,128,512]{2,1,0:T(8,128)(2,1)S(1)} %get-tuple-element.49), channel_id=1, source_target_pairs={{4,0},{8,4},{12,8},{5,1},{9,5},{13,9},{6,2},{10,6},{14,10},{7,3},{... | collective-permute-start | bytes 393224 | tf_op jit(solution)/shard_map/ppermute | solution.py:239
  58.9 1.3 %collective-permute-start.8 = (bf16[1,128,512]{2,1,0:T(8,128)(2,1)S(1)}, bf16[1,128,512]{2,1,0:T(8,128)(2,1)}, u32[]{:S(2)}, u32[]{:S(2)}) collective-permute-start(bf16[1,128,512]{2,1,0:T(8,128)(2,1)S(1)} %get-tuple-element.50), channel_id=1, source_target_pairs={{8,0},{12,4},{9,1},{13,5},{10,2},{14,6},{11,3},{15,7},{24,16},{28,... | collective-permute-start | bytes 393224 | tf_op jit(solution)/shard_map/ppermute | solution.py:239
  60.2 5.9 %collective-permute-done.1 = bf16[1,8,128,128]{3,2,1,0:T(8,128)(2,1)S(1)} collective-permute-done((bf16[1,8,128,128]{3,2,1,0:T(8,128)(2,1)S(1)}, bf16[1,8,128,128]{3,2,1,0:T(8,128)(2,1)S(1)}, u32[]{:S(2)}, u32[]{:S(2)}) %collective-permute-start.1) | collective-permute-done | bytes 262176 | tf_op jit(solution)/shard_map/ppermute | solution.py:239
  66.1 1.0 fusion.2
  67.1 1.3 %collective-permute-start.2 = (bf16[1,8,128,128]{3,2,1,0:T(8,128)(2,1)}, bf16[1,8,128,128]{3,2,1,0:T(8,128)(2,1)S(1)}, u32[]{:S(2)}, u32[]{:S(2)}) collective-permute-start(bf16[1,8,128,128]{3,2,1,0:T(8,128)(2,1)} %fusion.2), channel_id=1, source_target_pairs={{4,0},{8,4},{12,8},{5,1},{9,5},{13,9},{6,2},{10,6},{14,10},{7,3},{... | collective-permute-start | bytes 786440 | tf_op jit(solution)/shard_map/ppermute | solution.py:239
  68.4 0.0 reduce-scatter.2.cloned.1.call-done
  68.4 0.0 all-reduce.2.cloned.1.call-update
  68.4 3.2 %collective-permute-done.10 = bf16[1,128,512]{2,1,0:T(8,128)(2,1)} collective-permute-done((bf16[1,128,512]{2,1,0:T(8,128)(2,1)S(1)}, bf16[1,128,512]{2,1,0:T(8,128)(2,1)}, u32[]{:S(2)}, u32[]{:S(2)}) %collective-permute-start.10) | collective-permute-done | bytes 131104 | tf_op jit(solution)/shard_map/ppermute | solution.py:239
  71.7 0.0 collective-permute-done.9
  71.7 1.7 %add_convert_fusion = bf16[1,128,512]{2,1,0:T(8,128)(2,1)} fusion(bf16[1,128,512]{2,1,0:T(8,128)(2,1)} %collective-permute-done.10, bf16[1,128,512]{2,1,0:T(8,128)(2,1)} %collective-permute-done.9, bf16[1,128,512]{2,1,0:T(8,128)(2,1)S(1)} %get-tuple-element.51), kind=kLoop, calls=%fused_computation.11 | loop fusion | flops 393216 | bytes 524288 | tf_op jit(solution)/shard_map/convert_element_type | solution.py:329
  73.4 0.0 collective-permute-done.7
  73.4 14.9 %collective-permute-done.8 = bf16[1,128,512]{2,1,0:T(8,128)(2,1)} collective-permute-done((bf16[1,128,512]{2,1,0:T(8,128)(2,1)S(1)}, bf16[1,128,512]{2,1,0:T(8,128)(2,1)}, u32[]{:S(2)}, u32[]{:S(2)}) %collective-permute-start.8) | collective-permute-done | bytes 131104 | tf_op jit(solution)/shard_map/ppermute | solution.py:239
  88.3 1.7 %add_convert_fusion.1 = bf16[1,128,512]{2,1,0:T(8,128)(2,1)} fusion(bf16[1,128,512]{2,1,0:T(8,128)(2,1)} %collective-permute-done.8, bf16[1,128,512]{2,1,0:T(8,128)(2,1)S(1)} %collective-permute-done.7, bf16[1,128,512]{2,1,0:T(8,128)(2,1)S(1)} %get-tuple-element.48), kind=kLoop, calls=%fused_computation.12 | loop fusion | flops 393216 | bytes 524288 | tf_op jit(solution)/shard_map/convert_element_type | solution.py:329
  90.0 0.0 collective-permute-done.2
  90.1 0.0 copy-start.16
  90.1 0.0 copy-done.24
  90.1 0.0 copy-done.20
  90.1 0.0 copy-done.18
  90.1 0.0 copy-done.9
  90.1 0.0 copy-done.11
  90.1 0.9 copy-done
  91.1 0.1 copy-done.7
  91.1 1.0 copy-done.22
  92.2 5.6 %back.1 = (bf16[1,128,1024]{2,1,0:T(8,128)(2,1)}, bf16[1,128,1024]{2,1,0:T(8,128)(2,1)}, bf16[1,128,1024]{2,1,0:T(8,128)(2,1)}, f32[1,8,128]{2,1,0:T(8,128)}, f32[1,8,128]{2,1,0:T(8,128)}) custom-call(bf16[1,128,1024]{2,1,0:T(8,128)(2,1)S(1)} %copy-done.7, bf16[1,128,1024]{2,1,0:T(8,128)(2,1)S(1)} %copy-done.9, bf16[1,128,1024]{2,1,0:T(8,128)(2,1)S(1)} %copy-done.11, ...), custom_call_target="tpu_custom_call" | custom-call | flops 2013265920 | bytes 6291456 | tf_op jit(solution)/shard_map/back/pallas_call | solution.py:317
  97.7 13.6 %all-reduce.2.cloned.1.call-done = f32[16,64,128]{2,1,0:T(8,128)} async-done(((f32[16,64,128]{2,1,0:T(8,128)}), f32[16,64,128]{2,1,0:T(8,128)}) %all-reduce.2.cloned.1.call-update) | async-done | bytes 524304 | tf_op jit(solution)/shard_map/psum | solution.py:313
  111.3 1.9 %fusion.8 = (f32[8,64,128]{2,1,0:T(8,128)}, f32[8,64,128]{2,1,0:T(8,128)}) fusion(f32[16,64,128]{2,1,0:T(8,128)} %all-reduce.2.cloned.1.call-done), kind=kLoop, calls=%fused_computation.13 | loop fusion | bytes 1048576 | tf_op jit(solution)/shard_map/slice | solution.py:329
  (25 shorter events, 0.1 us)
Async XLA Ops:
  7.2 12.7 %copy-start.14 = (f32[1,8,128]{2,1,0:T(8,128)S(1)}, f32[1,8,128]{2,1,0:T(8,128)}, u32[]{:S(2)}) copy-start(f32[1,8,128]{2,1,0:T(8,128)} %gate_ref.3) | copy-start | bytes 12292
  7.2 61.2 %reduce-scatter.2.cloned.1.call-start = ((), (), s32[]{:S(2)}) async-start(), calls=%async_computation.1 | async-start | bytes 1572864 | tf_op jit(solution)/shard_map/reduce_scatter | solution.py:313
  7.2 30.6 %collective-permute-start.3 = (bf16[1,128,512]{2,1,0:T(8,128)(2,1)}, bf16[1,128,512]{2,1,0:T(8,128)(2,1)S(1)}, u32[]{:S(2)}, u32[]{:S(2)}) collective-permute-start(bf16[1,128,512]{2,1,0:T(8,128)(2,1)} %refs_2_.1), channel_id=1, source_target_pairs={{0,8},{4,12},{1,9},{5,13},{2,10},{6,14},{3,11},{7,15},{16,24},{20,... | collective-permute-start | bytes 393224 | tf_op jit(solution)/shard_map/ppermute | solution.py:239
  13.2 24.7 %collective-permute-start.4 = (bf16[1,128,512]{2,1,0:T(8,128)(2,1)}, bf16[1,128,512]{2,1,0:T(8,128)(2,1)S(1)}, u32[]{:S(2)}, u32[]{:S(2)}) collective-permute-start(bf16[1,128,512]{2,1,0:T(8,128)(2,1)} %refs_2_.1), channel_id=1, source_target_pairs={{0,4},{4,8},{8,12},{1,5},{5,9},{9,13},{2,6},{6,10},{10,14},{3,7},{... | collective-permute-start | bytes 393224 | tf_op jit(solution)/shard_map/ppermute | solution.py:239
  16.7 21.2 %collective-permute-start.5 = (bf16[1,128,512]{2,1,0:T(8,128)(2,1)}, bf16[1,128,512]{2,1,0:T(8,128)(2,1)S(1)}, u32[]{:S(2)}, u32[]{:S(2)}) collective-permute-start(bf16[1,128,512]{2,1,0:T(8,128)(2,1)} %refs_5_.1), channel_id=1, source_target_pairs={{0,8},{4,12},{1,9},{5,13},{2,10},{6,14},{3,11},{7,15},{16,24},{20,... | collective-permute-start | bytes 393224 | tf_op jit(solution)/shard_map/ppermute | solution.py:239
  18.0 19.9 %collective-permute-start.6 = (bf16[1,128,512]{2,1,0:T(8,128)(2,1)}, bf16[1,128,512]{2,1,0:T(8,128)(2,1)S(1)}, u32[]{:S(2)}, u32[]{:S(2)}) collective-permute-start(bf16[1,128,512]{2,1,0:T(8,128)(2,1)} %refs_5_.1), channel_id=1, source_target_pairs={{0,4},{4,8},{8,12},{1,5},{5,9},{9,13},{2,6},{6,10},{10,14},{3,7},{... | collective-permute-start | bytes 393224 | tf_op jit(solution)/shard_map/ppermute | solution.py:239
  19.9 1.0 copy-start.1
  20.9 0.9 copy-start.2
  21.8 0.9 copy-start.6
  22.8 0.9 copy-start.8
  23.7 0.9 copy-start.10
  24.7 0.7 copy-start.15
  25.4 12.5 %copy-start.3 = (bf16[1,128,1024]{2,1,0:T(8,128)(2,1)S(1)}, bf16[1,128,1024]{2,1,0:T(8,128)(2,1)}, u32[]{:S(2)}) copy-start(bf16[1,128,1024]{2,1,0:T(8,128)(2,1)} %q_ref.5) | copy-start | bytes 786436
  25.4 12.5 %copy-start.4 = (bf16[1,128,1024]{2,1,0:T(8,128)(2,1)S(1)}, bf16[1,128,1024]{2,1,0:T(8,128)(2,1)}, u32[]{:S(2)}) copy-start(bf16[1,128,1024]{2,1,0:T(8,128)(2,1)} %cot_ref.3) | copy-start | bytes 786436
  25.4 12.5 %copy-start.5 = (bf16[8,128,128]{2,1,0:T(8,128)(2,1)S(1)}, bf16[8,128,128]{2,1,0:T(8,128)(2,1)}, u32[]{:S(2)}) copy-start(bf16[8,128,128]{2,1,0:T(8,128)(2,1)} %rot_ref.3) | copy-start | bytes 786436
  25.4 12.5 %copy-start.12 = (bf16[1,128,512]{2,1,0:T(8,128)(2,1)S(1)}, bf16[1,128,512]{2,1,0:T(8,128)(2,1)}, u32[]{:S(2)}) copy-start(bf16[1,128,512]{2,1,0:T(8,128)(2,1)} %refs_2_.1) | copy-start | bytes 393220
  25.4 12.5 %copy-start.13 = (bf16[1,128,512]{2,1,0:T(8,128)(2,1)S(1)}, bf16[1,128,512]{2,1,0:T(8,128)(2,1)}, u32[]{:S(2)}) copy-start(bf16[1,128,512]{2,1,0:T(8,128)(2,1)} %refs_5_.1) | copy-start | bytes 393220
  35.6 0.8 copy-start.17
  36.4 0.8 copy-start.19
  37.2 0.7 copy-start.23
  37.9 4.9 %copy-start.21 = (f32[1,8,128,128]{3,2,1,0:T(8,128)}, f32[1,8,128,128]{3,2,1,0:T(8,128)S(1)}, u32[]{:S(2)}) copy-start(f32[1,8,128,128]{3,2,1,0:T(8,128)S(1)} %get-tuple-element.38.qs_ref) | copy-start | bytes 1572868
  43.9 67.5 %all-reduce.2.cloned.1.call-start = ((), (), s32[]{:S(2)}) async-start(), calls=%async_computation.2 | async-start | bytes 1048576 | tf_op jit(solution)/shard_map/psum | solution.py:313
  44.0 9.4 %collective-permute-start = (bf16[1,8,128,128]{3,2,1,0:T(8,128)(2,1)S(1)}, bf16[1,8,128,128]{3,2,1,0:T(8,128)(2,1)S(1)}, u32[]{:S(2)}, u32[]{:S(2)}) collective-permute-start(bf16[1,8,128,128]{3,2,1,0:T(8,128)(2,1)S(1)} %convert_element_type.38), channel_id=1, source_target_pairs={{4,0},{8,4},{12,8},{5,1},{9,5},{13,9},{6,2},{10,6},{14,10},{7,3},{... | collective-permute-start | bytes 786440 | tf_op jit(solution)/shard_map/ppermute | solution.py:239
  53.7 12.4 %collective-permute-start.1 = (bf16[1,8,128,128]{3,2,1,0:T(8,128)(2,1)S(1)}, bf16[1,8,128,128]{3,2,1,0:T(8,128)(2,1)S(1)}, u32[]{:S(2)}, u32[]{:S(2)}) collective-permute-start(bf16[1,8,128,128]{3,2,1,0:T(8,128)(2,1)S(1)} %fusion.3), channel_id=1, source_target_pairs={{4,0},{8,4},{12,8},{5,1},{9,5},{13,9},{6,2},{10,6},{14,10},{7,3},{... | collective-permute-start | bytes 786440 | tf_op jit(solution)/shard_map/ppermute | solution.py:239
  55.0 16.7 %collective-permute-start.10 = (bf16[1,128,512]{2,1,0:T(8,128)(2,1)S(1)}, bf16[1,128,512]{2,1,0:T(8,128)(2,1)}, u32[]{:S(2)}, u32[]{:S(2)}) collective-permute-start(bf16[1,128,512]{2,1,0:T(8,128)(2,1)S(1)} %get-tuple-element.53), channel_id=1, source_target_pairs={{8,0},{12,4},{9,1},{13,5},{10,2},{14,6},{11,3},{15,7},{24,16},{28,... | collective-permute-start | bytes 393224 | tf_op jit(solution)/shard_map/ppermute | solution.py:239
  56.3 15.4 %collective-permute-start.9 = (bf16[1,128,512]{2,1,0:T(8,128)(2,1)S(1)}, bf16[1,128,512]{2,1,0:T(8,128)(2,1)}, u32[]{:S(2)}, u32[]{:S(2)}) collective-permute-start(bf16[1,128,512]{2,1,0:T(8,128)(2,1)S(1)} %get-tuple-element.52), channel_id=1, source_target_pairs={{4,0},{8,4},{12,8},{5,1},{9,5},{13,9},{6,2},{10,6},{14,10},{7,3},{... | collective-permute-start | bytes 393224 | tf_op jit(solution)/shard_map/ppermute | solution.py:239
  57.6 15.8 %collective-permute-start.7 = (bf16[1,128,512]{2,1,0:T(8,128)(2,1)S(1)}, bf16[1,128,512]{2,1,0:T(8,128)(2,1)S(1)}, u32[]{:S(2)}, u32[]{:S(2)}) collective-permute-start(bf16[1,128,512]{2,1,0:T(8,128)(2,1)S(1)} %get-tuple-element.49), channel_id=1, source_target_pairs={{4,0},{8,4},{12,8},{5,1},{9,5},{13,9},{6,2},{10,6},{14,10},{7,3},{... | collective-permute-start | bytes 393224 | tf_op jit(solution)/shard_map/ppermute | solution.py:239
  58.9 29.5 %collective-permute-start.8 = (bf16[1,128,512]{2,1,0:T(8,128)(2,1)S(1)}, bf16[1,128,512]{2,1,0:T(8,128)(2,1)}, u32[]{:S(2)}, u32[]{:S(2)}) collective-permute-start(bf16[1,128,512]{2,1,0:T(8,128)(2,1)S(1)} %get-tuple-element.50), channel_id=1, source_target_pairs={{8,0},{12,4},{9,1},{13,5},{10,2},{14,6},{11,3},{15,7},{24,16},{28,... | collective-permute-start | bytes 393224 | tf_op jit(solution)/shard_map/ppermute | solution.py:239
  66.1 24.0 %copy-start.24 = (bf16[1,8,128,128]{3,2,1,0:T(8,128)(2,1)S(1)}, bf16[1,8,128,128]{3,2,1,0:T(8,128)(2,1)}, u32[]{:S(2)}) copy-start(bf16[1,8,128,128]{3,2,1,0:T(8,128)(2,1)} %copy-done.23) | copy-start | bytes 786436
  67.1 22.9 %collective-permute-start.2 = (bf16[1,8,128,128]{3,2,1,0:T(8,128)(2,1)}, bf16[1,8,128,128]{3,2,1,0:T(8,128)(2,1)S(1)}, u32[]{:S(2)}, u32[]{:S(2)}) collective-permute-start(bf16[1,8,128,128]{3,2,1,0:T(8,128)(2,1)} %fusion.2), channel_id=1, source_target_pairs={{4,0},{8,4},{12,8},{5,1},{9,5},{13,9},{6,2},{10,6},{14,10},{7,3},{... | collective-permute-start | bytes 786440 | tf_op jit(solution)/shard_map/ppermute | solution.py:239
  68.4 21.7 %copy-start.20 = (f32[1,8,128,128]{3,2,1,0:T(8,128)S(1)}, f32[1,8,128,128]{3,2,1,0:T(8,128)}, u32[]{:S(2)}) copy-start(f32[1,8,128,128]{3,2,1,0:T(8,128)} %copy-done.19) | copy-start | bytes 1572868
  71.7 18.4 %copy-start.18 = (f32[1,8,128,128]{3,2,1,0:T(8,128)S(1)}, f32[1,8,128,128]{3,2,1,0:T(8,128)}, u32[]{:S(2)}) copy-start(f32[1,8,128,128]{3,2,1,0:T(8,128)} %copy-done.17) | copy-start | bytes 1572868
  88.3 1.8 %copy-start.9 = (bf16[1,128,1024]{2,1,0:T(8,128)(2,1)S(1)}, bf16[1,128,1024]{2,1,0:T(8,128)(2,1)}, u32[]{:S(2)}) copy-start(bf16[1,128,1024]{2,1,0:T(8,128)(2,1)} %k_ref.3) | copy-start | bytes 786436
  88.3 1.8 %copy-start.11 = (bf16[1,128,1024]{2,1,0:T(8,128)(2,1)S(1)}, bf16[1,128,1024]{2,1,0:T(8,128)(2,1)}, u32[]{:S(2)}) copy-start(bf16[1,128,1024]{2,1,0:T(8,128)(2,1)} %v_ref.3) | copy-start | bytes 786436
  90.0 1.0 copy-start
  90.0 1.1 copy-start.7
  90.1 1.1 copy-start.16
  91.1 1.0 copy-start.22
Sparse Core Ops, SparseCore 0:
  44.0 18.5 reduce-scatter.1
  68.6 42.7 all-reduce.1

commit v2 on v1

--- a/solution.py
+++ b/solution.py
@@ -189,54 +189,216 @@
     lockstep(head(i) for i in range(per))
 
 
-def window_kernel(reach, group, place_ref, q_ref, cot_ref, rot_ref, *refs):
-    keys = jnp.concatenate([r[0] for r in refs[: reach + 1]], axis=0)
-    values = jnp.concatenate([r[0] for r in refs[reach + 1 : 2 * reach + 2]], axis=0)
-    dq_ref, term_ref = refs[2 * reach + 2 : 2 * reach + 4]
-    key_outs = refs[2 * reach + 4 : 3 * reach + 5]
-    value_outs = refs[3 * reach + 5 :]
+def middle_kernel(n, d_size, reach, group, travel, q_ref, cot_ref, rot_ref, k_ref, v_ref,
+                  local_ref, move_ref, gterm_ref,
+                  dq_ref, dk_ref, dv_ref, later_ref, share_ref,
+                  halo, carried, later, term_out, term_in, own_term, rot_all, rot_out, rot_in,
+                  part, part_out, part_in, final,
+                  halo_s, halo_r, chain_s, chain_r, term_s, term_r, rot_s, rot_r, ps, pr, fs, fr):
+    me, x = lax.axis_index("seq"), lax.axis_index("dp")
     rows = q_ref.shape[1]
+    heads = local_ref.shape[1]
+    kv_count = k_ref.shape[2] // 128
+    slab = 128 // d_size
+    piece = 2 * heads * slab // n
     scale = 128 ** (-0.5)
-    t = lax.broadcasted_iota(jnp.int32, (rows, keys.shape[0]), 0)
-    u = lax.broadcasted_iota(jnp.int32, (rows, keys.shape[0]), 1) - reach * rows
-    allowed = (u <= t) & (u > t - WINDOW) & (u + place_ref[0, 0] * rows >= 0)
-    key_sum, value_sum = [], []
-
-    def head(g):
-        lanes = slice(g * 128, (g + 1) * 128)
-        q, cot = q_ref[0, :, lanes], cot_ref[0, :, lanes]
-        out_grad = dot(cot, rot_ref[g], NN).astype(BF16)
-        scores = jnp.where(allowed, scale * dot(q, keys, NT), MASK_FLOOR)
-        yield
-        prob_grad = dot(out_grad, values, NT)
-        weights = jnp.exp(scores - jnp.max(scores, axis=1, keepdims=True))
-        probs = weights / jnp.sum(weights, axis=1, keepdims=True)
-        low = probs.astype(BF16)
-        yield
-        out = dot(low, values, NN)
-        row_dot = jnp.sum(probs * prob_grad, axis=1, keepdims=True)
-        dscore = (probs * (prob_grad - row_dot)).astype(BF16)
-        yield
-        dq_ref[0, :, lanes] = (scale * dot(dscore, keys, NN)).astype(BF16)
-        key_sum.append(dot(dscore, q, TN))
-        value_sum.append(dot(low, out_grad, TN))
-        term_ref[g] = dot(cot, out.astype(BF16), TN)
-
-    lockstep(head(g) for g in range(group))
-    key_term = (scale * functools.reduce(jnp.add, key_sum)).astype(BF16)
-    value_term = functools.reduce(jnp.add, value_sum).astype(BF16)
-    for j in range(reach + 1):
-        key_outs[j][0] = key_term[j * rows : (j + 1) * rows]
-        value_outs[j][0] = value_term[j * rows : (j + 1) * rows]
+
+    def remote(src, dst, send, recv, axis, peer):
+        return pltpu.make_async_remote_copy(
+            src_ref=src, dst_ref=dst, send_sem=send, recv_sem=recv,
+            device_id={axis: peer}, device_id_type=pl.DeviceIdType.MESH,
+        )
+
+    barrier = pltpu.get_barrier_semaphore()
+    for k in range(1, n):
+        pl.semaphore_signal(barrier, inc=1, device_id={"seq": lax.rem(me + k, n)},
+                            device_id_type=pl.DeviceIdType.MESH)
+    for k in range(1, d_size):
+        pl.semaphore_signal(barrier, inc=1, device_id={"dp": lax.rem(x + k, d_size)},
+                            device_id_type=pl.DeviceIdType.MESH)
+    pl.semaphore_wait(barrier, n - 1 + d_size - 1)
+
+    def halo_copy(d, j):
+        return remote((k_ref, v_ref)[j].at[0], halo.at[d - 1, j], halo_s.at[d - 1, j],
+                      halo_r.at[d - 1, j], "seq", lax.rem(me + d, n))
+
+    def chain_copy(h):
+        return remote(carried.at[h], later.at[h], chain_s.at[h], chain_r.at[h], "seq",
+                      lax.rem(me + n - 1, n))
+
+    def term_copy(d, j):
+        return remote(term_out.at[d - 1, j], term_in.at[d - 1, j], term_s.at[d - 1, j],
+                      term_r.at[d - 1, j], "seq", lax.rem(me + n - d, n))
+
+    def rot_copy(j, k):
+        peer = lax.rem(x + k, d_size)
+        at = pl.ds(pl.multiple_of(peer * slab, slab), slab)
+        return remote(rot_out.at[j, :, at, :], rot_in.at[k - 1, j],
+                      rot_s.at[k - 1, j], rot_r.at[k - 1, j], "dp", peer)
+
+    def piece_at(peer):
+        return pl.ds(pl.multiple_of(peer * piece, piece), piece)
+
+    def part_copy(k):
+        peer = lax.rem(me + k, n)
+        return remote(part_out.at[piece_at(peer)], part_in.at[k - 1], ps.at[k - 1], pr.at[k - 1],
+                      "seq", peer)
+
+    def final_copy(k):
+        peer = lax.rem(me + k, n)
+        return remote(final.at[0], final.at[k], fs.at[k - 1], fr.at[k - 1], "seq", peer)
+
+    for d in range(1, reach + 1):
+        @pl.when(me + d < n)
+        def _():
+            for j in range(2):
+                halo_copy(d, j).start()
+
+    @pl.when(me == n - 1)
+    def _():
+        later[...] = jnp.zeros_like(later)
+        for h in range(heads):
+            carried[h] = local_ref[0, h].astype(travel)
+            chain_copy(h).start()
+
+    rot_out[0] = gterm_ref[...].astype(BF16)
+    for k in range(1, d_size):
+        rot_copy(0, k).start()
+
+    for d in range(1, reach + 1):
+        @pl.when(me < d)
+        def _():
+            halo[d - 1] = jnp.zeros(halo.shape[1:], halo.dtype)
+
+        @pl.when(me >= d)
+        def _():
+            for j in range(2):
+                halo_copy(d, j).wait_recv()
+
+    span = (reach + 1) * rows
+    t = lax.broadcasted_iota(jnp.int32, (rows, span), 0)
+    u = lax.broadcasted_iota(jnp.int32, (rows, span), 1) - reach * rows
+    allowed = (u <= t) & (u > t - WINDOW) & (u + me * rows >= 0)
+
+    def key_head(c):
+        kv_lanes = slice(c * 128, (c + 1) * 128)
+        keys = jnp.concatenate(
+            [halo[d - 1, 0, :, kv_lanes] for d in range(reach, 0, -1)] + [k_ref[0, :, kv_lanes]], axis=0)
+        values = jnp.concatenate(
+            [halo[d - 1, 1, :, kv_lanes] for d in range(reach, 0, -1)] + [v_ref[0, :, kv_lanes]], axis=0)
+        key_sum, value_sum = 0.0, 0.0
+        for g in range(group):
+            head = c * group + g
+            lanes = slice(head * 128, (head + 1) * 128)
+            q, cot = q_ref[0, :, lanes], cot_ref[0, :, lanes]
+            out_grad = dot(cot, rot_ref[head], NN).astype(BF16)
+            scores = jnp.where(allowed, scale * dot(q, keys, NT), MASK_FLOOR)
+            yield
+            prob_grad = dot(out_grad, values, NT)
+            weights = jnp.exp(scores - jnp.max(scores, axis=1, keepdims=True))
+            probs = weights / jnp.sum(weights, axis=1, keepdims=True)
+            low = probs.astype(BF16)
+            yield
+            out = dot(low, values, NN)
+            row_dot = jnp.sum(probs * prob_grad, axis=1, keepdims=True)
+            dscore = (probs * (prob_grad - row_dot)).astype(BF16)
+            yield
+            dq_ref[0, :, lanes] = (scale * dot(dscore, keys, NN)).astype(BF16)
+            key_sum += dot(dscore, q, TN)
+            value_sum += dot(low, out_grad, TN)
+            term = dot(cot, out.astype(BF16), TN)
+            rot_all[head] = term
+            rot_out[1, head] = term.astype(BF16)
+            yield
+        for j, whole in enumerate(((scale * key_sum).astype(BF16), value_sum.astype(BF16))):
+            for d in range(1, reach + 1):
+                term_out[d - 1, j, :, kv_lanes] = whole[(reach - d) * rows : (reach - d + 1) * rows]
+            own_term[j, :, kv_lanes] = whole[reach * rows :]
+
+    lockstep(key_head(c) for c in range(kv_count))
+    for k in range(1, d_size):
+        rot_copy(1, k).start()
+
+    for h in range(heads):
+        @pl.when(me < n - 1)
+        def _():
+            chain_copy(h).wait_recv()
+
+            @pl.when(me > 0)
+            def _():
+                carried[h] = (local_ref[0, h] + mm(later[h].astype(F32), move_ref[0, h], NN)).astype(travel)
+                chain_copy(h).start()
+
+    for d in range(1, reach + 1):
+        @pl.when(me >= d)
+        def _():
+            for j in range(2):
+                term_copy(d, j).start()
+
+    own = pl.ds(pl.multiple_of(x * slab, slab), slab)
+    for j, terms in enumerate((gterm_ref, rot_all)):
+        for k in range(1, d_size):
+            rot_copy(j, k).wait_recv()
+        total = terms[:, own, :]
+        for k in range(1, d_size):
+            total = total + rot_in[k - 1, j].astype(F32)
+        flat = total.reshape(heads * slab, 128)
+        part[j * heads * slab : (j + 1) * heads * slab] = flat
+        part_out[j * heads * slab : (j + 1) * heads * slab] = flat.astype(BF16)
+    for k in range(1, n):
+        part_copy(k).start()
+    later_ref[0] = later[...].astype(F32)
+    for k in range(1, n):
+        part_copy(k).wait_recv()
+    mine = part[piece_at(me)]
+    for k in range(1, n):
+        mine = mine + part_in[k - 1].astype(F32)
+    final[0] = mine.astype(BF16)
+    share_ref[piece_at(me)] = mine
+    for k in range(1, n):
+        final_copy(k).start()
+
+    for j, out in enumerate((dk_ref, dv_ref)):
+        for d in range(1, reach + 1):
+            @pl.when(me + d < n)
+            def _():
+                term_copy(d, j).wait_recv()
+
+            @pl.when(me + d >= n)
+            def _():
+                term_in[d - 1, j] = jnp.zeros(term_in.shape[2:], BF16)
+        total = own_term[j].astype(F32)
+        for d in range(1, reach + 1):
+            total = total + term_in[d - 1, j].astype(F32)
+        out[0] = total.astype(BF16)
+
+    for k in range(1, n):
+        final_copy(k).wait_recv()
+        share_ref[piece_at(lax.rem(me + n - k, n))] = final[k].astype(F32)
+
+    for k in range(1, n):
+        part_copy(k).wait_send()
+        final_copy(k).wait_send()
+    for j in range(2):
+        for k in range(1, d_size):
+            rot_copy(j, k).wait_send()
+        for d in range(1, reach + 1):
+            @pl.when(me + d < n)
+            def _():
+                halo_copy(d, j).wait_send()
+
+            @pl.when(me >= d)
+            def _():
+                term_copy(d, j).wait_send()
+
+    @pl.when(me > 0)
+    def _():
+        for h in range(heads):
+            chain_copy(h).wait_send()
 
 
 def per_head(shape, per):
     return pl.BlockSpec((1, per) + shape, lambda b, h: (b, h, 0, 0))
-
-
-def shifted(x, by):
-    size = lax.axis_size("seq")
-    return lax.ppermute(x, "seq", [(i, i + by) for i in range(size) if 0 <= i + by < size])
 
 
 def body(gdn_query, gdn_key, gdn_value, gdn_cot, gate_log, beta, state_in, gdn_rot,
@@ -252,9 +414,6 @@
     params = pltpu.CompilerParams(vmem_limit_bytes=48 * 2**20)
     flops = 2 * heads * 128**3
 
-    keys = [shifted(att_key, d) for d in range(reach, 0, -1)] + [att_key]
-    values = [shifted(att_value, d) for d in range(reach, 0, -1)] + [att_value]
-
     tok = pl.BlockSpec((1, tokens, per * 128), lambda b, h: (b, 0, h))
     gate_spec = pl.BlockSpec((1, heads, tokens), lambda b, h: (b, 0, 0))
     state_spec = pl.BlockSpec((1, 1, per, 128, 128), lambda b, h: (b, 0, h, 0, 0))
@@ -277,40 +436,42 @@
     )(gdn_query, gdn_key, gdn_value, gdn_cot, gate_log, beta, state_in, gdn_rot)
 
     travel = BF16 if n_seq <= 8 else F32
-    later = shifted(local.astype(travel), -1)
-    for _ in range(n_seq - 2):
-        carried = local + jnp.einsum(
-            "bhvk,bhkl->bhvl", later.astype(F32), move, precision=lax.Precision.HIGH
-        )
-        later = shifted(carried.astype(travel), -1)
-    later = later.astype(F32)
-
-    q_spec = pl.BlockSpec((1, tokens, group * 128), lambda b, h: (b, 0, h))
-    kv_spec = pl.BlockSpec((1, tokens, 128), lambda b, h: (b, 0, h))
-    group_spec = pl.BlockSpec((group, 128, 128), lambda b, h: (h, 0, 0))
+    d_size = lax.axis_size("dp")
+    slab = 128 // d_size
+    piece = 2 * heads * slab // n_seq
+    vmem = pl.BlockSpec(memory_space=pltpu.VMEM)
+    sem = pltpu.SemaphoreType.DMA
     kv_out = like(rows_s, tokens, kv_width, dtype=BF16)
-    place = jnp.full((1, 1), lax.axis_index("seq"), jnp.int32)
-    outs = pl.pallas_call(
-        functools.partial(window_kernel, reach, group),
-        name="window",
-        grid=(rows_s, kv_count),
-        in_specs=[pl.BlockSpec(memory_space=pltpu.SMEM), q_spec, q_spec, group_spec]
-        + [kv_spec] * (2 * reach + 2),
-        out_specs=[q_spec, group_spec] + [kv_spec] * (2 * reach + 2),
-        out_shape=[like(rows_s, tokens, width, dtype=BF16), like(heads, 128, 128)]
-        + [kv_out] * (2 * reach + 2),
-        compiler_params=params,
-        cost_estimate=pl.CostEstimate(flops=60 * flops, bytes_accessed=4 * 2**20, transcendentals=0),
-    )(place, att_query, att_cot, att_rot, *keys, *values)
-    att_dq, att_term = outs[:2]
-    key_terms, value_terms = outs[2 : reach + 3], outs[reach + 3 :]
-    dk, dv = key_terms[reach].astype(F32), value_terms[reach].astype(F32)
-    for d in range(1, reach + 1):
-        dk = dk + shifted(key_terms[reach - d], -d).astype(F32)
-        dv = dv + shifted(value_terms[reach - d], -d).astype(F32)
-
-    both = jnp.concatenate([gdn_term, att_term], axis=0)
-    share = lax.psum(lax.psum_scatter(both, "dp", scatter_dimension=1, tiled=True), "seq")
+    att_dq, dk, dv, later, share = pl.pallas_call(
+        functools.partial(middle_kernel, n_seq, d_size, reach, group, travel),
+        name="middle",
+        in_specs=[vmem] * 8,
+        out_specs=[vmem] * 5,
+        out_shape=[like(rows_s, tokens, width, dtype=BF16), kv_out, kv_out, mat,
+                   like(2 * heads * slab, 128)],
+        scratch_shapes=[
+            pltpu.VMEM((reach, 2, tokens, kv_width), BF16),
+            pltpu.VMEM((heads, 128, 128), travel),
+            pltpu.VMEM((heads, 128, 128), travel),
+            pltpu.VMEM((reach, 2, tokens, kv_width), BF16),
+            pltpu.VMEM((reach, 2, tokens, kv_width), BF16),
+            pltpu.VMEM((2, tokens, kv_width), BF16),
+            pltpu.VMEM((heads, 128, 128), F32),
+            pltpu.VMEM((2, heads, 128, 128), BF16),
+            pltpu.VMEM((d_size - 1, 2, heads, slab, 128), BF16),
+            pltpu.VMEM((2 * heads * slab, 128), F32),
+            pltpu.VMEM((2 * heads * slab, 128), BF16),
+            pltpu.VMEM((n_seq - 1, piece, 128), BF16),
+            pltpu.VMEM((n_seq, piece, 128), BF16),
+            sem((reach, 2)), sem((reach, 2)), sem((heads,)), sem((heads,)),
+            sem((reach, 2)), sem((reach, 2)), sem((d_size - 1, 2)), sem((d_size - 1, 2)),
+            sem((n_seq - 1,)), sem((n_seq - 1,)), sem((n_seq - 1,)), sem((n_seq - 1,)),
+        ],
+        compiler_params=pltpu.CompilerParams(
+            collective_id=0, has_side_effects=True, vmem_limit_bytes=48 * 2**20
+        ),
+    )(att_query, att_cot, att_rot, att_key, att_value, local, move, gdn_term)
+    share = share.reshape(2 * heads, slab, 128)
 
     dq_spec = like(rows_s, tokens, width, dtype=BF16)
     gates = like(rows_s, heads, tokens)
@@ -326,7 +487,7 @@
     )(gdn_query, gdn_key, gdn_value, gate_log, beta, state_in, later, w, y, z, ks, qs, grad)
 
     return (gdn_dq, gdn_dk, gdn_dv, dgate, dbeta, share[:heads],
-            att_dq, dk.astype(BF16), dv.astype(BF16), share[heads:])
+            att_dq, dk, dv, share[heads:])
 
 
 def solution(mesh):

time: 121 us -> 84 us (0.69)
  Pallas kernels: 20.6 us -> 73.1 us
  waiting for transfers between devices: 45.8 us -> 0 us
  starting transfers between devices: 21.8 us -> 0 us
  between operations: 14.4 us -> 0.79 us
  other arithmetic: 4.57 us -> 0 us
  local copies, waits for them, and re-layouts: 11.7 us -> 9.74 us
  matrix products: 1.33 us -> 0 us
    pallas_call x1, Pallas kernels: 4.83 us -> 57.5 us  [body(): pl.pallas_call(functools.partial(middle_kernel, n_seq, d_size, reach, gro...]
    ppermute x11 -> x0, waiting for transfers between devices: 32.1 us -> none  [shifted(): lax.ppermute(x, 'seq', [(i, i + by) for i in range(size) if 0 <= i + by <...]
    ppermute x11 -> x0, starting transfers between devices: 21.7 us -> none  [shifted(): lax.ppermute(x, 'seq', [(i, i + by) for i in range(size) if 0 <= i + by <...]
    psum x1 -> x0, waiting for transfers between devices: 13.6 us -> none  [body(): lax.psum(lax.psum_scatter(both, 'dp', scatter_dimension=1, tiled=True), '...]
    convert_element_type x4 -> x0, other arithmetic: 3.5 us -> none  [the longest x1 1.74 us: body(): dv.astype(BF16)]
    dot_general x2 -> x0, matrix products: 1.33 us -> none  [body(): jnp.einsum('bhvk,bhkl->bhvl', later.astype(F32), move, precision=lax.Prec...]
    unnamed x50 -> x33, local copies, waits for them, and re-layouts: 9.82 us -> 8.91 us
  transfers between devices with their start and end apart: 13 -> 0, of which waited for: 5 -> 0; matrix products, arithmetic and copies ran while one was open for 4% -> 0% of each run, Pallas kernels for 13% -> 0%
where the time goes in v2:
time: 84 us; the launch traced here: 83.7 us
  Pallas kernels  73.1 us (87%)
  local copies, waits for them, and re-layouts  9.74 us (12%)
    pallas_call x1, Pallas kernels, body(): pl.pallas_call(functools.partial(middle_kernel, n_seq, d_size, reach, gro...  57.5 us
    pallas_call x1, Pallas kernels, body(): pl.pallas_call(functools.partial(ahead_kernel, per), name='ahead', grid=(...  10.1 us
    unnamed x33, local copies, waits for them, and re-layouts  8.91 us
    pallas_call x1, Pallas kernels, body(): pl.pallas_call(functools.partial(back_kernel, per), name='back', grid=(ro...  5.54 us

profile of v2, /device:TPU:0, one launch (start us, length us, event | category | flops | bytes accessed | tf_op | source)
XLA Modules:
  0.0 83.7 jit_solution(16027213153168979681)
XLA Ops:
  0.6 0.0 copy-start.2
  0.7 0.0 copy-start.1
  0.7 0.0 copy-start.4
  0.7 0.0 copy-start.3
  0.7 0.0 copy-start
  0.7 0.0 copy-start.6
  0.7 1.0 %copy-done.6 = bf16[1,128,1024]{2,1,0:T(8,128)(2,1)S(1)} copy-done((bf16[1,128,1024]{2,1,0:T(8,128)(2,1)S(1)}, bf16[1,128,1024]{2,1,0:T(8,128)(2,1)}, u32[]{:S(2)}) %copy-start.6) | copy-done | bytes 262168
  1.7 0.0 copy-start.7
  1.7 0.9 %copy-done.7 = bf16[8,128,128]{2,1,0:T(8,128)(2,1)S(1)} copy-done((bf16[8,128,128]{2,1,0:T(8,128)(2,1)S(1)}, bf16[8,128,128]{2,1,0:T(8,128)(2,1)}, u32[]{:S(2)}) %copy-start.7) | copy-done | bytes 262168
  2.7 0.0 copy-start.8
  2.7 0.9 %copy-done.8 = bf16[1,128,1024]{2,1,0:T(8,128)(2,1)S(1)} copy-done((bf16[1,128,1024]{2,1,0:T(8,128)(2,1)S(1)}, bf16[1,128,1024]{2,1,0:T(8,128)(2,1)}, u32[]{:S(2)}) %copy-start.8) | copy-done | bytes 262168
  3.6 0.0 copy-start.9
  3.6 0.9 %copy-done.9 = bf16[1,128,1024]{2,1,0:T(8,128)(2,1)S(1)} copy-done((bf16[1,128,1024]{2,1,0:T(8,128)(2,1)S(1)}, bf16[1,128,1024]{2,1,0:T(8,128)(2,1)}, u32[]{:S(2)}) %copy-start.9) | copy-done | bytes 262168
  4.6 0.0 copy-start.10
  4.6 0.9 %copy-done.10 = bf16[1,128,1024]{2,1,0:T(8,128)(2,1)S(1)} copy-done((bf16[1,128,1024]{2,1,0:T(8,128)(2,1)S(1)}, bf16[1,128,1024]{2,1,0:T(8,128)(2,1)}, u32[]{:S(2)}) %copy-start.10) | copy-done | bytes 262168
  5.5 0.0 copy-start.11
  5.5 0.7 copy-done.11
  6.2 0.0 copy-start.13
  6.2 0.7 copy-done.13
  6.9 10.1 %ahead.1 = (f32[1,8,128,128]{3,2,1,0:T(8,128)S(1)}, f32[1,8,128,128]{3,2,1,0:T(8,128)S(1)}, f32[1,8,128,128]{3,2,1,0:T(8,128)S(1)}, f32[1,8,128,128]{3,2,1,0:T(8...) custom-call(bf16[1,128,1024]{2,1,0:T(8,128)(2,1)S(1)} %copy-done.8, ...), custom_call_target="tpu_custom_call" | custom-call | flops 2684354560 | bytes 6291456 | tf_op jit(solution)/shard_map/ahead/pallas_call | solution.py:426
  17.0 0.0 copy-done.2
  17.0 0.0 copy-done.1
  17.0 0.0 copy-done.4
  17.0 0.0 copy-done.3
  17.0 0.0 copy-done
  17.0 0.0 copy-start.5
  17.0 57.5 %middle.1 = (bf16[1,128,1024]{2,1,0:T(8,128)(2,1)S(1)}, bf16[1,128,512]{2,1,0:T(8,128)(2,1)S(1)}, bf16[1,128,512]{2,1,0:T(8,128)(2,1)S(1)}, f32[1,8,128,128]{3,2,1,0:T(8,128)S(1)}, f32[1024,128]{1,0:T(8,128)S(1)}) custom-call(bf16[1,128,1024]{2,1,0:T(8,128)(2,1)S(1)} %copy-done, bf16[1,128,1024]{2,1,0:T(8,128)(2,1)S(1)} %copy-done.1, ...), custom_call_target="tpu_custom_call" | custom-call | tf_op jit(solution)/shard_map/middle/pallas_call | solution.py:445
  74.6 0.0 copy-start.14
  74.6 0.0 copy-start.12
  74.6 0.0 copy-done.5
  74.6 0.7 copy-done.14
  75.3 0.0 copy-done.12
  75.3 5.5 %back.1 = (bf16[1,128,1024]{2,1,0:T(8,128)(2,1)}, bf16[1,128,1024]{2,1,0:T(8,128)(2,1)}, bf16[1,128,1024]{2,1,0:T(8,128)(2,1)}, f32[1,8,128]{2,1,0:T(8,128)}, f32[1,8,128]{2,1,0:T(8,128)}) custom-call(bf16[1,128,1024]{2,1,0:T(8,128)(2,1)S(1)} %copy-done.8, bf16[1,128,1024]{2,1,0:T(8,128)(2,1)S(1)} %copy-done.9, bf16[1,128,1024]{2,1,0:T(8,128)(2,1)S(1)} %copy-done.10, ...), custom_call_target="tpu_custom_call" | custom-call | flops 2013265920 | bytes 6291456 | tf_op jit(solution)/shard_map/back/pallas_call | solution.py:478
  80.8 0.8 fusion
  81.6 0.7 copy.26
  82.3 0.7 copy.27
  83.0 0.7 copy.28
Async XLA Ops:
  0.6 16.3 %copy-start.2 = (bf16[8,128,128]{2,1,0:T(8,128)(2,1)S(1)}, bf16[8,128,128]{2,1,0:T(8,128)(2,1)}, u32[]{:S(2)}) copy-start(bf16[8,128,128]{2,1,0:T(8,128)(2,1)} %rot_ref.3) | copy-start | bytes 786436
  0.7 16.3 %copy-start.1 = (bf16[1,128,1024]{2,1,0:T(8,128)(2,1)S(1)}, bf16[1,128,1024]{2,1,0:T(8,128)(2,1)}, u32[]{:S(2)}) copy-start(bf16[1,128,1024]{2,1,0:T(8,128)(2,1)} %cot_ref.3) | copy-start | bytes 786436
  0.7 16.3 %copy-start.4 = (bf16[1,128,512]{2,1,0:T(8,128)(2,1)S(1)}, bf16[1,128,512]{2,1,0:T(8,128)(2,1)}, u32[]{:S(2)}) copy-start(bf16[1,128,512]{2,1,0:T(8,128)(2,1)} %v_ref.4) | copy-start | bytes 393220
  0.7 16.3 %copy-start.3 = (bf16[1,128,512]{2,1,0:T(8,128)(2,1)S(1)}, bf16[1,128,512]{2,1,0:T(8,128)(2,1)}, u32[]{:S(2)}) copy-start(bf16[1,128,512]{2,1,0:T(8,128)(2,1)} %k_ref.4) | copy-start | bytes 393220
  0.7 16.3 %copy-start = (bf16[1,128,1024]{2,1,0:T(8,128)(2,1)S(1)}, bf16[1,128,1024]{2,1,0:T(8,128)(2,1)}, u32[]{:S(2)}) copy-start(bf16[1,128,1024]{2,1,0:T(8,128)(2,1)} %q_ref.4) | copy-start | bytes 786436
  0.7 1.0 %copy-start.6 = (bf16[1,128,1024]{2,1,0:T(8,128)(2,1)S(1)}, bf16[1,128,1024]{2,1,0:T(8,128)(2,1)}, u32[]{:S(2)}) copy-start(bf16[1,128,1024]{2,1,0:T(8,128)(2,1)} %cot_ref.2) | copy-start | bytes 786436
  1.7 0.9 %copy-start.7 = (bf16[8,128,128]{2,1,0:T(8,128)(2,1)S(1)}, bf16[8,128,128]{2,1,0:T(8,128)(2,1)}, u32[]{:S(2)}) copy-start(bf16[8,128,128]{2,1,0:T(8,128)(2,1)} %rot_ref.2) | copy-start | bytes 786436
  2.7 0.9 %copy-start.8 = (bf16[1,128,1024]{2,1,0:T(8,128)(2,1)S(1)}, bf16[1,128,1024]{2,1,0:T(8,128)(2,1)}, u32[]{:S(2)}) copy-start(bf16[1,128,1024]{2,1,0:T(8,128)(2,1)} %q_ref.5) | copy-start | bytes 786436
  3.6 0.9 %copy-start.9 = (bf16[1,128,1024]{2,1,0:T(8,128)(2,1)S(1)}, bf16[1,128,1024]{2,1,0:T(8,128)(2,1)}, u32[]{:S(2)}) copy-start(bf16[1,128,1024]{2,1,0:T(8,128)(2,1)} %k_ref.5) | copy-start | bytes 786436
  4.6 0.9 %copy-start.10 = (bf16[1,128,1024]{2,1,0:T(8,128)(2,1)S(1)}, bf16[1,128,1024]{2,1,0:T(8,128)(2,1)}, u32[]{:S(2)}) copy-start(bf16[1,128,1024]{2,1,0:T(8,128)(2,1)} %v_ref.5) | copy-start | bytes 786436
  5.5 0.7 copy-start.11
  6.2 0.7 copy-start.13
  17.0 57.6 %copy-start.5 = (f32[1,1,8,128,128]{4,3,2,1,0:T(8,128)S(1)}, f32[1,1,8,128,128]{4,3,2,1,0:T(8,128)}, u32[]{:S(2)}) copy-start(f32[1,1,8,128,128]{4,3,2,1,0:T(8,128)} %state_ref.3) | copy-start | bytes 1572868
  74.6 0.7 copy-start.14
  74.6 0.7 copy-start.12

commit v3 on v2

--- a/solution.py
+++ b/solution.py
@@ -81,15 +81,13 @@
     )
 
 
-def ahead_kernel(per, q_ref, k_ref, v_ref, cot_ref, gate_ref, beta_ref, state_ref, rot_ref,
+def ahead_heads(chosen, q_ref, k_ref, v_ref, cot_ref, gate_ref, beta_ref, state_ref, rot_ref,
                  local_ref, move_ref, w_ref, y_ref, z_ref, ks_ref, qs_ref, grad_ref, term_ref):
-    first = pl.program_id(1) * per
-
     def head(i):
         lanes = slice(i * 128, (i + 1) * 128)
         q, k, v, cot = (r[0, :, lanes] for r in (q_ref, k_ref, v_ref, cot_ref))
-        gate = gate_ref[0, pl.ds(first + i, 1), :]
-        beta = beta_ref[0, pl.ds(first + i, 1), :]
+        gate = gate_ref[0, i : i + 1, :]
+        beta = beta_ref[0, i : i + 1, :]
         out_grad = dot(cot, rot_ref[i], NN).astype(BF16)
         grad_ref[0, i] = out_grad
         f = token_facts(q, k, gate, beta)
@@ -136,7 +134,7 @@
         og = f["decay"] * out_grad.astype(F32)
         local_ref[0, i] = mm(og, f["qn"], TN) - mm(bd * y, f["kn"], TN)
 
-    lockstep(head(i) for i in range(per))
+    lockstep(head(i) for i in chosen)
 
 
 def back_kernel(per, q_ref, k_ref, v_ref, gate_ref, beta_ref, state_ref,
@@ -189,15 +187,16 @@
     lockstep(head(i) for i in range(per))
 
 
-def middle_kernel(n, d_size, reach, group, travel, q_ref, cot_ref, rot_ref, k_ref, v_ref,
+def middle_kernel(n, d_size, reach, group, per, travel, q_ref, cot_ref, rot_ref, k_ref, v_ref,
+                  gq_ref, gk_ref, gv_ref, gcot_ref, gate_ref, beta_ref, state_ref, grot_ref,
+                  dq_ref, dk_ref, dv_ref, later_ref, share_ref, w_ref, y_ref, z_ref, ks_ref, qs_ref, grad_ref,
                   local_ref, move_ref, gterm_ref,
-                  dq_ref, dk_ref, dv_ref, later_ref, share_ref,
                   halo, carried, later, term_out, term_in, own_term, rot_all, rot_out, rot_in,
                   part, part_out, part_in, final,
                   halo_s, halo_r, chain_s, chain_r, term_s, term_r, rot_s, rot_r, ps, pr, fs, fr):
     me, x = lax.axis_index("seq"), lax.axis_index("dp")
     rows = q_ref.shape[1]
-    heads = local_ref.shape[1]
+    heads = state_ref.shape[2]
     kv_count = k_ref.shape[2] // 128
     slab = 128 // d_size
     piece = 2 * heads * slab // n
@@ -253,6 +252,11 @@
         def _():
             for j in range(2):
                 halo_copy(d, j).start()
+
+    for first in range(0, heads, per):
+        ahead_heads(range(first, first + per), gq_ref, gk_ref, gv_ref, gcot_ref, gate_ref, beta_ref,
+                    state_ref, grot_ref, local_ref, move_ref, w_ref, y_ref, z_ref, ks_ref, qs_ref,
+                    grad_ref, gterm_ref)
 
     @pl.when(me == n - 1)
     def _():
@@ -423,18 +427,6 @@
     wide = like(rows_s, heads, tokens, 128)
     mat = like(rows_s, heads, 128, 128)
 
-    local, move, w, y, z, ks, qs, grad, gdn_term = pl.pallas_call(
-        functools.partial(ahead_kernel, per),
-        name="ahead",
-        grid=(rows_s, heads // per),
-        in_specs=[tok] * 4 + [gate_spec] * 2 + [state_spec, rot_spec],
-        out_specs=[square] * 2 + [token_wide] * 6 + [rot_spec],
-        out_shape=[mat, mat, wide, wide, wide, wide, wide,
-                   like(rows_s, heads, tokens, 128, dtype=BF16), like(heads, 128, 128)],
-        compiler_params=params,
-        cost_estimate=pl.CostEstimate(flops=80 * flops, bytes_accessed=6 * 2**20, transcendentals=0),
-    )(gdn_query, gdn_key, gdn_value, gdn_cot, gate_log, beta, state_in, gdn_rot)
-
     travel = BF16 if n_seq <= 8 else F32
     d_size = lax.axis_size("dp")
     slab = 128 // d_size
@@ -442,14 +434,18 @@
     vmem = pl.BlockSpec(memory_space=pltpu.VMEM)
     sem = pltpu.SemaphoreType.DMA
     kv_out = like(rows_s, tokens, kv_width, dtype=BF16)
-    att_dq, dk, dv, later, share = pl.pallas_call(
-        functools.partial(middle_kernel, n_seq, d_size, reach, group, travel),
+    att_dq, dk, dv, later, share, w, y, z, ks, qs, grad = pl.pallas_call(
+        functools.partial(middle_kernel, n_seq, d_size, reach, group, per, travel),
         name="middle",
-        in_specs=[vmem] * 8,
-        out_specs=[vmem] * 5,
+        in_specs=[vmem] * 13,
+        out_specs=[vmem] * 11,
         out_shape=[like(rows_s, tokens, width, dtype=BF16), kv_out, kv_out, mat,
-                   like(2 * heads * slab, 128)],
+                   like(2 * heads * slab, 128), wide, wide, wide, wide, wide,
+                   like(rows_s, heads, tokens, 128, dtype=BF16)],
         scratch_shapes=[
+            pltpu.VMEM((1, heads, 128, 128), F32),
+            pltpu.VMEM((1, heads, 128, 128), F32),
+            pltpu.VMEM((heads, 128, 128), F32),
             pltpu.VMEM((reach, 2, tokens, kv_width), BF16),
             pltpu.VMEM((heads, 128, 128), travel),
             pltpu.VMEM((heads, 128, 128), travel),
@@ -470,7 +466,8 @@
         compiler_params=pltpu.CompilerParams(
             collective_id=0, has_side_effects=True, vmem_limit_bytes=48 * 2**20
         ),
-    )(att_query, att_cot, att_rot, att_key, att_value, local, move, gdn_term)
+    )(att_query, att_cot, att_rot, att_key, att_value,
+      gdn_query, gdn_key, gdn_value, gdn_cot, gate_log, beta, state_in, gdn_rot)
     share = share.reshape(2 * heads, slab, 128)
 
     dq_spec = like(rows_s, tokens, width, dtype=BF16)

time: 84 us -> 82.8 us (0.986)
  Pallas kernels: 73.1 us -> 65.1 us
  local copies, waits for them, and re-layouts: 9.74 us -> 16.4 us
    pallas_call x1 -> x0, Pallas kernels: 10.1 us -> none  [body(): pl.pallas_call(functools.partial(ahead_kernel, per), name='ahead', grid=(...]
    unnamed x33 -> x41, local copies, waits for them, and re-layouts: 8.91 us -> 15.6 us
    pallas_call x1, Pallas kernels: 57.5 us -> 59.6 us  [body(): pl.pallas_call(functools.partial(middle_kernel, n_seq, d_size, reach, gro...]
where the time goes in v3:
time: 82.8 us; the launch traced here: 82.2 us
  Pallas kernels  65.1 us (79%)
  local copies, waits for them, and re-layouts  16.4 us (20%)
    pallas_call x1, Pallas kernels, body(): pl.pallas_call(functools.partial(middle_kernel, n_seq, d_size, reach, gro...  59.6 us
    unnamed x41, local copies, waits for them, and re-layouts  15.6 us
    pallas_call x1, Pallas kernels, body(): pl.pallas_call(functools.partial(back_kernel, per), name='back', grid=(ro...  5.54 us

profile of v3, /device:TPU:0, one launch (start us, length us, event | category | flops | bytes accessed | tf_op | source)
XLA Modules:
  0.0 82.2 jit_solution(7774433323755023943)
XLA Ops:
  0.6 0.0 copy-start
  0.7 0.0 copy-start.1
  0.7 1.0 %copy-done.1 = bf16[1,128,1024]{2,1,0:T(8,128)(2,1)S(1)} copy-done((bf16[1,128,1024]{2,1,0:T(8,128)(2,1)S(1)}, bf16[1,128,1024]{2,1,0:T(8,128)(2,1)}, u32[]{:S(2)}) %copy-start.1) | copy-done | bytes 262168
  1.7 0.0 copy-start.2
  1.7 0.9 %copy-done.2 = bf16[1,128,1024]{2,1,0:T(8,128)(2,1)S(1)} copy-done((bf16[1,128,1024]{2,1,0:T(8,128)(2,1)S(1)}, bf16[1,128,1024]{2,1,0:T(8,128)(2,1)}, u32[]{:S(2)}) %copy-start.2) | copy-done | bytes 262168
  2.6 0.0 copy-start.3
  2.6 0.9 %copy-done.3 = bf16[8,128,128]{2,1,0:T(8,128)(2,1)S(1)} copy-done((bf16[8,128,128]{2,1,0:T(8,128)(2,1)S(1)}, bf16[8,128,128]{2,1,0:T(8,128)(2,1)}, u32[]{:S(2)}) %copy-start.3) | copy-done | bytes 262168
  3.6 0.0 copy-start.4
  3.6 0.9 %copy-done.4 = bf16[1,128,1024]{2,1,0:T(8,128)(2,1)S(1)} copy-done((bf16[1,128,1024]{2,1,0:T(8,128)(2,1)S(1)}, bf16[1,128,1024]{2,1,0:T(8,128)(2,1)}, u32[]{:S(2)}) %copy-start.4) | copy-done | bytes 262168
  4.5 0.0 copy-start.5
  4.5 0.9 %copy-done.5 = bf16[8,128,128]{2,1,0:T(8,128)(2,1)S(1)} copy-done((bf16[8,128,128]{2,1,0:T(8,128)(2,1)S(1)}, bf16[8,128,128]{2,1,0:T(8,128)(2,1)}, u32[]{:S(2)}) %copy-start.5) | copy-done | bytes 262168
  5.5 0.0 copy-start.6
  5.5 0.9 %copy-done.6 = bf16[1,128,1024]{2,1,0:T(8,128)(2,1)S(1)} copy-done((bf16[1,128,1024]{2,1,0:T(8,128)(2,1)S(1)}, bf16[1,128,1024]{2,1,0:T(8,128)(2,1)}, u32[]{:S(2)}) %copy-start.6) | copy-done | bytes 262168
  6.4 0.0 copy-start.7
  6.4 0.9 %copy-done.7 = bf16[1,128,1024]{2,1,0:T(8,128)(2,1)S(1)} copy-done((bf16[1,128,1024]{2,1,0:T(8,128)(2,1)S(1)}, bf16[1,128,1024]{2,1,0:T(8,128)(2,1)}, u32[]{:S(2)}) %copy-start.7) | copy-done | bytes 262168
  7.4 0.0 copy-start.9
  7.4 0.9 %copy-done.9 = bf16[1,128,1024]{2,1,0:T(8,128)(2,1)S(1)} copy-done((bf16[1,128,1024]{2,1,0:T(8,128)(2,1)S(1)}, bf16[1,128,1024]{2,1,0:T(8,128)(2,1)}, u32[]{:S(2)}) %copy-start.9) | copy-done | bytes 262168
  8.3 0.0 copy-start.11
  8.3 0.9 %copy-done.11 = bf16[1,128,512]{2,1,0:T(8,128)(2,1)S(1)} copy-done((bf16[1,128,512]{2,1,0:T(8,128)(2,1)S(1)}, bf16[1,128,512]{2,1,0:T(8,128)(2,1)}, u32[]{:S(2)}) %copy-start.11) | copy-done | bytes 131096
  9.2 0.0 copy-start.12
  9.2 0.9 %copy-done.12 = bf16[1,128,512]{2,1,0:T(8,128)(2,1)S(1)} copy-done((bf16[1,128,512]{2,1,0:T(8,128)(2,1)S(1)}, bf16[1,128,512]{2,1,0:T(8,128)(2,1)}, u32[]{:S(2)}) %copy-start.12) | copy-done | bytes 131096
  10.1 0.0 copy-start.13
  10.1 0.7 copy-done.13
  10.8 0.0 copy-start.15
  10.8 0.7 copy-done.15
  11.5 0.0 copy-start.8
  11.5 0.0 copy-start.10
  11.5 59.6 %middle.1 = (bf16[1,128,1024]{2,1,0:T(8,128)(2,1)S(1)}, bf16[1,128,512]{2,1,0:T(8,128)(2,1)S(1)}, bf16[1,128,512]{2,1,0:T(8,128)(2,1)S(1)}, f32[1,8,128,128]{3,2...) custom-call(bf16[1,128,1024]{2,1,0:T(8,128)(2,1)S(1)} %copy-done.1, ...), custom_call_target="tpu_custom_call" | custom-call | tf_op jit(solution)/shard_map/middle/pallas_call | solution.py:437
  71.1 0.0 copy-start.16
  71.1 0.0 copy-start.14
  71.1 0.0 copy-done
  71.1 0.0 copy-done.8
  71.1 0.0 copy-done.10
  71.1 0.6 copy-done.16
  71.8 0.0 copy-done.14
  71.8 0.0 copy-start.17
  71.8 1.0 %copy-done.17 = f32[1,8,128,128]{3,2,1,0:T(8,128)S(1)} copy-done((f32[1,8,128,128]{3,2,1,0:T(8,128)S(1)}, f32[1,8,128,128]{3,2,1,0:T(8,128)}, u32[]{:S(2)}) %copy-start.17) | copy-done | bytes 524312
  72.8 0.0 copy-start.18
  72.8 1.0 %copy-done.18 = f32[1,8,128,128]{3,2,1,0:T(8,128)S(1)} copy-done((f32[1,8,128,128]{3,2,1,0:T(8,128)S(1)}, f32[1,8,128,128]{3,2,1,0:T(8,128)}, u32[]{:S(2)}) %copy-start.18) | copy-done | bytes 524312
  73.9 5.5 %back.1 = (bf16[1,128,1024]{2,1,0:T(8,128)(2,1)}, bf16[1,128,1024]{2,1,0:T(8,128)(2,1)}, bf16[1,128,1024]{2,1,0:T(8,128)(2,1)}, f32[1,8,128]{2,1,0:T(8,128)}, f32[1,8,128]{2,1,0:T(8,128)}) custom-call(bf16[1,128,1024]{2,1,0:T(8,128)(2,1)S(1)} %copy-done.6, bf16[1,128,1024]{2,1,0:T(8,128)(2,1)S(1)} %copy-done.8, bf16[1,128,1024]{2,1,0:T(8,128)(2,1)S(1)} %copy-done.10, ...), custom_call_target="tpu_custom_call" | custom-call | flops 2013265920 | bytes 6291456 | tf_op jit(solution)/shard_map/back/pallas_call | solution.py:475
  79.4 0.8 %fusion = (f32[512,128]{1,0:T(8,128)}, f32[512,128]{1,0:T(8,128)}) fusion(f32[1024,128]{1,0:T(8,128)S(1)} %get-tuple-element.38), kind=kLoop, calls=%fused_computation | loop fusion | bytes 1048576 | tf_op jit(solution)/shard_map/slice | solution.py:487
  80.2 0.7 copy.26
  80.9 0.7 copy.27
  81.6 0.7 copy.28
Async XLA Ops:
  0.6 70.4 %copy-start = (f32[1,1,8,128,128]{4,3,2,1,0:T(8,128)S(1)}, f32[1,1,8,128,128]{4,3,2,1,0:T(8,128)}, u32[]{:S(2)}) copy-start(f32[1,1,8,128,128]{4,3,2,1,0:T(8,128)} %state_ref.3) | copy-start | bytes 1572868
  0.7 1.0 %copy-start.1 = (bf16[1,128,1024]{2,1,0:T(8,128)(2,1)S(1)}, bf16[1,128,1024]{2,1,0:T(8,128)(2,1)}, u32[]{:S(2)}) copy-start(bf16[1,128,1024]{2,1,0:T(8,128)(2,1)} %q_ref.2) | copy-start | bytes 786436
  1.7 0.9 %copy-start.2 = (bf16[1,128,1024]{2,1,0:T(8,128)(2,1)S(1)}, bf16[1,128,1024]{2,1,0:T(8,128)(2,1)}, u32[]{:S(2)}) copy-start(bf16[1,128,1024]{2,1,0:T(8,128)(2,1)} %cot_ref.1) | copy-start | bytes 786436
  2.6 0.9 %copy-start.3 = (bf16[8,128,128]{2,1,0:T(8,128)(2,1)S(1)}, bf16[8,128,128]{2,1,0:T(8,128)(2,1)}, u32[]{:S(2)}) copy-start(bf16[8,128,128]{2,1,0:T(8,128)(2,1)} %rot_ref.1) | copy-start | bytes 786436
  3.6 0.9 %copy-start.4 = (bf16[1,128,1024]{2,1,0:T(8,128)(2,1)S(1)}, bf16[1,128,1024]{2,1,0:T(8,128)(2,1)}, u32[]{:S(2)}) copy-start(bf16[1,128,1024]{2,1,0:T(8,128)(2,1)} %gcot_ref.1) | copy-start | bytes 786436
  4.5 0.9 %copy-start.5 = (bf16[8,128,128]{2,1,0:T(8,128)(2,1)S(1)}, bf16[8,128,128]{2,1,0:T(8,128)(2,1)}, u32[]{:S(2)}) copy-start(bf16[8,128,128]{2,1,0:T(8,128)(2,1)} %grot_ref.1) | copy-start | bytes 786436
  5.5 0.9 %copy-start.6 = (bf16[1,128,1024]{2,1,0:T(8,128)(2,1)S(1)}, bf16[1,128,1024]{2,1,0:T(8,128)(2,1)}, u32[]{:S(2)}) copy-start(bf16[1,128,1024]{2,1,0:T(8,128)(2,1)} %q_ref.3) | copy-start | bytes 786436
  6.4 0.9 %copy-start.7 = (bf16[1,128,1024]{2,1,0:T(8,128)(2,1)S(1)}, bf16[1,128,1024]{2,1,0:T(8,128)(2,1)}, u32[]{:S(2)}) copy-start(bf16[1,128,1024]{2,1,0:T(8,128)(2,1)} %k_ref.3) | copy-start | bytes 786436
  7.4 0.9 %copy-start.9 = (bf16[1,128,1024]{2,1,0:T(8,128)(2,1)S(1)}, bf16[1,128,1024]{2,1,0:T(8,128)(2,1)}, u32[]{:S(2)}) copy-start(bf16[1,128,1024]{2,1,0:T(8,128)(2,1)} %v_ref.3) | copy-start | bytes 786436
  8.3 0.9 %copy-start.11 = (bf16[1,128,512]{2,1,0:T(8,128)(2,1)S(1)}, bf16[1,128,512]{2,1,0:T(8,128)(2,1)}, u32[]{:S(2)}) copy-start(bf16[1,128,512]{2,1,0:T(8,128)(2,1)} %k_ref.2) | copy-start | bytes 393220
  9.2 0.9 %copy-start.12 = (bf16[1,128,512]{2,1,0:T(8,128)(2,1)S(1)}, bf16[1,128,512]{2,1,0:T(8,128)(2,1)}, u32[]{:S(2)}) copy-start(bf16[1,128,512]{2,1,0:T(8,128)(2,1)} %v_ref.2) | copy-start | bytes 393220
  10.1 0.7 copy-start.13
  10.8 0.7 copy-start.15
  11.5 59.6 %copy-start.8 = (bf16[1,128,1024]{2,1,0:T(8,128)(2,1)S(1)}, bf16[1,128,1024]{2,1,0:T(8,128)(2,1)}, u32[]{:S(2)}) copy-start(bf16[1,128,1024]{2,1,0:T(8,128)(2,1)} %k_ref.3) | copy-start | bytes 786436
  11.5 59.6 %copy-start.10 = (bf16[1,128,1024]{2,1,0:T(8,128)(2,1)S(1)}, bf16[1,128,1024]{2,1,0:T(8,128)(2,1)}, u32[]{:S(2)}) copy-start(bf16[1,128,1024]{2,1,0:T(8,128)(2,1)} %v_ref.3) | copy-start | bytes 786436
  71.1 0.7 copy-start.16
  71.1 0.7 copy-start.14
  71.8 1.0 %copy-start.17 = (f32[1,8,128,128]{3,2,1,0:T(8,128)S(1)}, f32[1,8,128,128]{3,2,1,0:T(8,128)}, u32[]{:S(2)}) copy-start(f32[1,8,128,128]{3,2,1,0:T(8,128)} %get-tuple-element.30.ks_ref) | copy-start | bytes 1572868
  72.8 1.0 %copy-start.18 = (f32[1,8,128,128]{3,2,1,0:T(8,128)S(1)}, f32[1,8,128,128]{3,2,1,0:T(8,128)}, u32[]{:S(2)}) copy-start(f32[1,8,128,128]{3,2,1,0:T(8,128)} %get-tuple-element.31.qs_ref) | copy-start | bytes 1572868

commit v4 on v3

--- a/solution.py
+++ b/solution.py
@@ -323,21 +323,21 @@
     for k in range(1, d_size):
         rot_copy(1, k).start()
 
-    for h in range(heads):
-        @pl.when(me < n - 1)
-        def _():
-            chain_copy(h).wait_recv()
-
-            @pl.when(me > 0)
-            def _():
-                carried[h] = (local_ref[0, h] + mm(later[h].astype(F32), move_ref[0, h], NN)).astype(travel)
-                chain_copy(h).start()
-
     for d in range(1, reach + 1):
         @pl.when(me >= d)
         def _():
             for j in range(2):
                 term_copy(d, j).start()
+
+    for h in range(heads):
+        @pl.when(me < n - 1)
+        def _():
+            chain_copy(h).wait_recv()
+
+            @pl.when(me > 0)
+            def _():
+                carried[h] = (local_ref[0, h] + mm(later[h].astype(F32), move_ref[0, h], NN)).astype(travel)
+                chain_copy(h).start()
 
     own = pl.ds(pl.multiple_of(x * slab, slab), slab)
     for j, terms in enumerate((gterm_ref, rot_all)):

time: 82.8 us -> 89.5 us (1.081)
  Pallas kernels: 65.1 us -> 71.8 us
    pallas_call x1, Pallas kernels: 59.6 us -> 66.2 us  [body(): pl.pallas_call(functools.partial(middle_kernel, n_seq, d_size, reach, gro...]
where the time goes in v4:
time: 89.5 us; the launch traced here: 88.9 us
  Pallas kernels  71.8 us (80%)
  local copies, waits for them, and re-layouts  16.4 us (18%)
    pallas_call x1, Pallas kernels, body(): pl.pallas_call(functools.partial(middle_kernel, n_seq, d_size, reach, gro...  66.2 us
    unnamed x41, local copies, waits for them, and re-layouts  15.6 us
    pallas_call x1, Pallas kernels, body(): pl.pallas_call(functools.partial(back_kernel, per), name='back', grid=(ro...  5.54 us

profile of v4, /device:TPU:0, one launch (start us, length us, event | category | flops | bytes accessed | tf_op | source)
XLA Modules:
  0.0 88.9 jit_solution(4611540010643156940)
XLA Ops:
  0.6 0.0 copy-start
  0.7 0.0 copy-start.1
  0.7 1.0 %copy-done.1 = bf16[1,128,1024]{2,1,0:T(8,128)(2,1)S(1)} copy-done((bf16[1,128,1024]{2,1,0:T(8,128)(2,1)S(1)}, bf16[1,128,1024]{2,1,0:T(8,128)(2,1)}, u32[]{:S(2)}) %copy-start.1) | copy-done | bytes 262168
  1.7 0.0 copy-start.2
  1.7 0.9 %copy-done.2 = bf16[1,128,1024]{2,1,0:T(8,128)(2,1)S(1)} copy-done((bf16[1,128,1024]{2,1,0:T(8,128)(2,1)S(1)}, bf16[1,128,1024]{2,1,0:T(8,128)(2,1)}, u32[]{:S(2)}) %copy-start.2) | copy-done | bytes 262168
  2.6 0.0 copy-start.3
  2.6 0.9 %copy-done.3 = bf16[8,128,128]{2,1,0:T(8,128)(2,1)S(1)} copy-done((bf16[8,128,128]{2,1,0:T(8,128)(2,1)S(1)}, bf16[8,128,128]{2,1,0:T(8,128)(2,1)}, u32[]{:S(2)}) %copy-start.3) | copy-done | bytes 262168
  3.6 0.0 copy-start.4
  3.6 0.9 %copy-done.4 = bf16[1,128,1024]{2,1,0:T(8,128)(2,1)S(1)} copy-done((bf16[1,128,1024]{2,1,0:T(8,128)(2,1)S(1)}, bf16[1,128,1024]{2,1,0:T(8,128)(2,1)}, u32[]{:S(2)}) %copy-start.4) | copy-done | bytes 262168
  4.5 0.0 copy-start.5
  4.5 0.9 %copy-done.5 = bf16[8,128,128]{2,1,0:T(8,128)(2,1)S(1)} copy-done((bf16[8,128,128]{2,1,0:T(8,128)(2,1)S(1)}, bf16[8,128,128]{2,1,0:T(8,128)(2,1)}, u32[]{:S(2)}) %copy-start.5) | copy-done | bytes 262168
  5.5 0.0 copy-start.6
  5.5 0.9 %copy-done.6 = bf16[1,128,1024]{2,1,0:T(8,128)(2,1)S(1)} copy-done((bf16[1,128,1024]{2,1,0:T(8,128)(2,1)S(1)}, bf16[1,128,1024]{2,1,0:T(8,128)(2,1)}, u32[]{:S(2)}) %copy-start.6) | copy-done | bytes 262168
  6.4 0.0 copy-start.7
  6.4 0.9 %copy-done.7 = bf16[1,128,1024]{2,1,0:T(8,128)(2,1)S(1)} copy-done((bf16[1,128,1024]{2,1,0:T(8,128)(2,1)S(1)}, bf16[1,128,1024]{2,1,0:T(8,128)(2,1)}, u32[]{:S(2)}) %copy-start.7) | copy-done | bytes 262168
  7.4 0.0 copy-start.9
  7.4 0.9 %copy-done.9 = bf16[1,128,1024]{2,1,0:T(8,128)(2,1)S(1)} copy-done((bf16[1,128,1024]{2,1,0:T(8,128)(2,1)S(1)}, bf16[1,128,1024]{2,1,0:T(8,128)(2,1)}, u32[]{:S(2)}) %copy-start.9) | copy-done | bytes 262168
  8.3 0.0 copy-start.11
  8.3 0.9 %copy-done.11 = bf16[1,128,512]{2,1,0:T(8,128)(2,1)S(1)} copy-done((bf16[1,128,512]{2,1,0:T(8,128)(2,1)S(1)}, bf16[1,128,512]{2,1,0:T(8,128)(2,1)}, u32[]{:S(2)}) %copy-start.11) | copy-done | bytes 131096
  9.2 0.0 copy-start.12
  9.2 0.9 %copy-done.12 = bf16[1,128,512]{2,1,0:T(8,128)(2,1)S(1)} copy-done((bf16[1,128,512]{2,1,0:T(8,128)(2,1)S(1)}, bf16[1,128,512]{2,1,0:T(8,128)(2,1)}, u32[]{:S(2)}) %copy-start.12) | copy-done | bytes 131096
  10.1 0.0 copy-start.13
  10.1 0.7 copy-done.13
  10.8 0.0 copy-start.15
  10.8 0.7 copy-done.15
  11.5 0.0 copy-start.8
  11.5 0.0 copy-start.10
  11.5 66.2 %middle.1 = (bf16[1,128,1024]{2,1,0:T(8,128)(2,1)S(1)}, bf16[1,128,512]{2,1,0:T(8,128)(2,1)S(1)}, bf16[1,128,512]{2,1,0:T(8,128)(2,1)S(1)}, f32[1,8,128,128]{3,2...) custom-call(bf16[1,128,1024]{2,1,0:T(8,128)(2,1)S(1)} %copy-done.1, ...), custom_call_target="tpu_custom_call" | custom-call | tf_op jit(solution)/shard_map/middle/pallas_call | solution.py:437
  77.7 0.0 copy-start.16
  77.7 0.0 copy-start.14
  77.8 0.0 copy-done
  77.8 0.0 copy-done.8
  77.8 0.0 copy-done.10
  77.8 0.6 copy-done.16
  78.4 0.0 copy-done.14
  78.4 0.0 copy-start.17
  78.4 1.0 %copy-done.17 = f32[1,8,128,128]{3,2,1,0:T(8,128)S(1)} copy-done((f32[1,8,128,128]{3,2,1,0:T(8,128)S(1)}, f32[1,8,128,128]{3,2,1,0:T(8,128)}, u32[]{:S(2)}) %copy-start.17) | copy-done | bytes 524312
  79.5 0.0 copy-start.18
  79.5 1.0 %copy-done.18 = f32[1,8,128,128]{3,2,1,0:T(8,128)S(1)} copy-done((f32[1,8,128,128]{3,2,1,0:T(8,128)S(1)}, f32[1,8,128,128]{3,2,1,0:T(8,128)}, u32[]{:S(2)}) %copy-start.18) | copy-done | bytes 524312
  80.5 5.5 %back.1 = (bf16[1,128,1024]{2,1,0:T(8,128)(2,1)}, bf16[1,128,1024]{2,1,0:T(8,128)(2,1)}, bf16[1,128,1024]{2,1,0:T(8,128)(2,1)}, f32[1,8,128]{2,1,0:T(8,128)}, f32[1,8,128]{2,1,0:T(8,128)}) custom-call(bf16[1,128,1024]{2,1,0:T(8,128)(2,1)S(1)} %copy-done.6, bf16[1,128,1024]{2,1,0:T(8,128)(2,1)S(1)} %copy-done.8, bf16[1,128,1024]{2,1,0:T(8,128)(2,1)S(1)} %copy-done.10, ...), custom_call_target="tpu_custom_call" | custom-call | flops 2013265920 | bytes 6291456 | tf_op jit(solution)/shard_map/back/pallas_call | solution.py:475
  86.1 0.8 fusion
  86.9 0.7 copy.26
  87.6 0.7 copy.27
  88.2 0.7 copy.28
Async XLA Ops:
  0.6 77.1 %copy-start = (f32[1,1,8,128,128]{4,3,2,1,0:T(8,128)S(1)}, f32[1,1,8,128,128]{4,3,2,1,0:T(8,128)}, u32[]{:S(2)}) copy-start(f32[1,1,8,128,128]{4,3,2,1,0:T(8,128)} %state_ref.3) | copy-start | bytes 1572868
  0.7 1.0 %copy-start.1 = (bf16[1,128,1024]{2,1,0:T(8,128)(2,1)S(1)}, bf16[1,128,1024]{2,1,0:T(8,128)(2,1)}, u32[]{:S(2)}) copy-start(bf16[1,128,1024]{2,1,0:T(8,128)(2,1)} %q_ref.2) | copy-start | bytes 786436
  1.7 0.9 %copy-start.2 = (bf16[1,128,1024]{2,1,0:T(8,128)(2,1)S(1)}, bf16[1,128,1024]{2,1,0:T(8,128)(2,1)}, u32[]{:S(2)}) copy-start(bf16[1,128,1024]{2,1,0:T(8,128)(2,1)} %cot_ref.1) | copy-start | bytes 786436
  2.6 0.9 %copy-start.3 = (bf16[8,128,128]{2,1,0:T(8,128)(2,1)S(1)}, bf16[8,128,128]{2,1,0:T(8,128)(2,1)}, u32[]{:S(2)}) copy-start(bf16[8,128,128]{2,1,0:T(8,128)(2,1)} %rot_ref.1) | copy-start | bytes 786436
  3.6 0.9 %copy-start.4 = (bf16[1,128,1024]{2,1,0:T(8,128)(2,1)S(1)}, bf16[1,128,1024]{2,1,0:T(8,128)(2,1)}, u32[]{:S(2)}) copy-start(bf16[1,128,1024]{2,1,0:T(8,128)(2,1)} %gcot_ref.1) | copy-start | bytes 786436
  4.5 0.9 %copy-start.5 = (bf16[8,128,128]{2,1,0:T(8,128)(2,1)S(1)}, bf16[8,128,128]{2,1,0:T(8,128)(2,1)}, u32[]{:S(2)}) copy-start(bf16[8,128,128]{2,1,0:T(8,128)(2,1)} %grot_ref.1) | copy-start | bytes 786436
  5.5 0.9 %copy-start.6 = (bf16[1,128,1024]{2,1,0:T(8,128)(2,1)S(1)}, bf16[1,128,1024]{2,1,0:T(8,128)(2,1)}, u32[]{:S(2)}) copy-start(bf16[1,128,1024]{2,1,0:T(8,128)(2,1)} %q_ref.3) | copy-start | bytes 786436
  6.4 0.9 %copy-start.7 = (bf16[1,128,1024]{2,1,0:T(8,128)(2,1)S(1)}, bf16[1,128,1024]{2,1,0:T(8,128)(2,1)}, u32[]{:S(2)}) copy-start(bf16[1,128,1024]{2,1,0:T(8,128)(2,1)} %k_ref.3) | copy-start | bytes 786436
  7.4 0.9 %copy-start.9 = (bf16[1,128,1024]{2,1,0:T(8,128)(2,1)S(1)}, bf16[1,128,1024]{2,1,0:T(8,128)(2,1)}, u32[]{:S(2)}) copy-start(bf16[1,128,1024]{2,1,0:T(8,128)(2,1)} %v_ref.3) | copy-start | bytes 786436
  8.3 0.9 %copy-start.11 = (bf16[1,128,512]{2,1,0:T(8,128)(2,1)S(1)}, bf16[1,128,512]{2,1,0:T(8,128)(2,1)}, u32[]{:S(2)}) copy-start(bf16[1,128,512]{2,1,0:T(8,128)(2,1)} %k_ref.2) | copy-start | bytes 393220
  9.2 0.9 %copy-start.12 = (bf16[1,128,512]{2,1,0:T(8,128)(2,1)S(1)}, bf16[1,128,512]{2,1,0:T(8,128)(2,1)}, u32[]{:S(2)}) copy-start(bf16[1,128,512]{2,1,0:T(8,128)(2,1)} %v_ref.2) | copy-start | bytes 393220
  10.1 0.7 copy-start.13
  10.8 0.7 copy-start.15
  11.5 66.3 %copy-start.8 = (bf16[1,128,1024]{2,1,0:T(8,128)(2,1)S(1)}, bf16[1,128,1024]{2,1,0:T(8,128)(2,1)}, u32[]{:S(2)}) copy-start(bf16[1,128,1024]{2,1,0:T(8,128)(2,1)} %k_ref.3) | copy-start | bytes 786436
  11.5 66.3 %copy-start.10 = (bf16[1,128,1024]{2,1,0:T(8,128)(2,1)S(1)}, bf16[1,128,1024]{2,1,0:T(8,128)(2,1)}, u32[]{:S(2)}) copy-start(bf16[1,128,1024]{2,1,0:T(8,128)(2,1)} %v_ref.3) | copy-start | bytes 786436
  77.7 0.7 copy-start.16
  77.7 0.7 copy-start.14
  78.4 1.0 %copy-start.17 = (f32[1,8,128,128]{3,2,1,0:T(8,128)S(1)}, f32[1,8,128,128]{3,2,1,0:T(8,128)}, u32[]{:S(2)}) copy-start(f32[1,8,128,128]{3,2,1,0:T(8,128)} %get-tuple-element.30.ks_ref) | copy-start | bytes 1572868
  79.5 1.0 %copy-start.18 = (f32[1,8,128,128]{3,2,1,0:T(8,128)S(1)}, f32[1,8,128,128]{3,2,1,0:T(8,128)}, u32[]{:S(2)}) copy-start(f32[1,8,128,128]{3,2,1,0:T(8,128)} %get-tuple-element.31.qs_ref) | copy-start | bytes 1572868
